TPU v7x, 256 devices: a whole 4x4x8 slice. The times are simulated.
256 devices in a mesh: dp: 8 (over z_hi, core), expert: 32 (over z_lo, x, y).
Axes of the slice: x: 4, y: 4, z: 8 (z_hi: 4, z_lo: 2; z = z_hi * 2 + z_lo), core: 2. Of those that a mesh axis runs over, the one named last changes fastest.
Arguments:
- tokens: bfloat16 [4096, 4096], P('expert', 'dp'), may hold values from -6 to 6
- gates: float32 [4096, 8], P('expert'), may hold values from 0.03 to 0.5
- expert_ids: int32 [4096, 8], P('expert'), may hold values from 0 to 31, as said below
- d_mixed: bfloat16 [4096, 4096], P('expert', 'dp'), may hold values from -6 to 6
- w_up: bfloat16 [32, 4096, 1024], P('expert', 'dp'), may hold values from -0.09375 to 0.09375
- w_down: bfloat16 [32, 1024, 4096], P('expert', None, 'dp'), may hold values from -0.1875 to 0.1875
Outputs:
- mixed: bfloat16 [4096, 4096], P('expert', 'dp')
- d_tokens: bfloat16 [4096, 4096], P('expert', 'dp')
- grad_up: bfloat16 [32, 4096, 1024], P('expert', 'dp')
- grad_down: bfloat16 [32, 1024, 4096], P('expert', None, 'dp')
Inputs may be any that keep to these rules, and one draw needn't show every extreme that they name: `expert_ids`: each row names 8 different experts. In the tokens of one device (aligned blocks of 128 rows) one expert, the same for every device, is named by exactly 64 tokens, and every other expert by at most 31 tokens; both bounds are reached on every device.
All inputs are finite; a program needn't handle non-finite values.
Results may differ from a plain program's by a relative error of at most 0.025.
Values may be sent and summed in bfloat16 or wider, within the bound.
No kernel may reach another device: no remote copies, remote signals or barrier semaphores. Data moves between devices by JAX's collectives and lax.ppermute only.
A program may use at most 64 MiB of HBM per device.

v0:
```python
import jax
import jax.numpy as jnp
from jax import lax
from jax.experimental import pallas as pl
from jax.experimental.pallas import tpu as pltpu
from jax.sharding import PartitionSpec as P

F32 = jnp.float32
BF16 = jnp.bfloat16
PLANES = [list(range(16)), list(range(16, 32))]
PARTNER = [(e, e ^ 16) for e in range(32)]
SIBLING = [(j, j ^ 1) for j in range(8)]


def ring(step):
    return [(j, ((j // 2 + step) % 4) * 2 + j % 2) for j in range(8)]


PLUS, MINUS = ring(1), ring(-1)


def mm(left, right, left_dim, right_dim):
    dims = (((left_dim,), (right_dim,)), ((), ()))
    return lax.dot_general(left, right, dims, preferred_element_type=F32)


def exchange(payload):
    return lax.all_to_all(payload, "expert", split_axis=0, concat_axis=0, tiled=True)


def exchange_in_plane(payload):
    return lax.all_to_all(
        payload, "expert", split_axis=0, concat_axis=0, tiled=True, axis_index_groups=PLANES
    )


def partner(block):
    return lax.ppermute(block, "expert", PARTNER)


def send(block, pairs):
    return lax.ppermute(block, "dp", pairs)


def add16(left, right):
    return (left.astype(F32) + right.astype(F32)).astype(BF16)


def after(*values):
    return lax.optimization_barrier(values)


def pick(blocks, index, axis=0):
    return lax.dynamic_index_in_dim(blocks, index, axis, keepdims=False)


def params():
    return pltpu.CompilerParams(vmem_limit_bytes=40 * 1024 * 1024)


def dispatch(spot, gate, tokens, mixed):
    groups, rows = spot.shape
    width = tokens.shape[1]
    step = 8

    def body(spot_ref, gate_ref, token_ref, mixed_ref, out_ref):
        at = lax.broadcasted_iota(jnp.int32, (step, 32, rows), 1)
        hit = at == spot_ref[...]
        scale = jnp.sum(jnp.where(hit, gate_ref[...], 0.0).reshape(step * 32, rows), 1, keepdims=True)
        one = jnp.where(hit, 1.0, 0.0).reshape(step * 32, rows).astype(BF16)
        out_ref[:, :width] = mm(one, token_ref[...], 1, 0).astype(BF16)
        out_ref[:, width:] = (scale * mm(one, mixed_ref[...], 1, 0)).astype(BF16)

    line = pl.BlockSpec((step, 1, rows), lambda e: (e, 0, 0))
    whole = pl.BlockSpec((rows, width), lambda e: (0, 0))
    return pl.pallas_call(
        body,
        grid=(groups // step,),
        in_specs=[line, line, whole, whole],
        out_specs=pl.BlockSpec((32 * step, 2 * width), lambda e: (e, 0)),
        out_shape=jax.ShapeDtypeStruct((32 * groups, 2 * width), BF16),
        compiler_params=params(),
    )(spot[:, None], gate[:, None], tokens, mixed)


ORDER = ((0, 2), (1, 1), (1, 2), (0, 3), (0, 1), (1, 3), (0, 0), (1, 0))


def parts_for_sibling(rows, up, down):
    def body(row_ref, up_ref, down_ref, out_ref):
        product = (
            mm(row_ref[:, :512], up_ref[...], 1, 0).astype(BF16),
            mm(row_ref[:, 512:], down_ref[...], 1, 1).astype(BF16),
        )
        for i, (which, block) in enumerate(ORDER):
            out_ref[i] = product[which][128 * block : 128 * block + 128]

    return pl.pallas_call(
        body,
        out_shape=jax.ShapeDtypeStruct((8, 128, 1024), BF16),
        compiler_params=params(),
    )(rows, up, down)


def parts_with_sibling(rows, up, down, came):
    def body(row_ref, up_ref, down_ref, came_ref, *out_refs):
        product = (
            mm(row_ref[:, :512], up_ref[...], 1, 0),
            mm(row_ref[:, 512:], down_ref[...], 1, 1),
        )
        for i, (which, block) in enumerate(ORDER):
            part = product[which][128 * block : 128 * block + 128]
            out_refs[i // 2][i % 2] = (part + came_ref[i].astype(F32)).astype(BF16)

    return pl.pallas_call(
        body,
        out_shape=[jax.ShapeDtypeStruct((2, 128, 1024), BF16)] * 4,
        compiler_params=params(),
    )(rows, up, down, came)


def sum_over_features(own, other, up, down):
    came = send(parts_for_sibling(other, up, down), SIBLING)
    first_up, first_down, second, here = parts_with_sibling(own, up, down, came)
    got_up, got_down = after(send(first_up, PLUS), send(first_down, MINUS))
    next_up, next_down, got_up, got_down, here = after(
        add16(second[0], got_up[0]), add16(second[1], got_down[0]), got_up, got_down, here
    )
    up_second = send(next_up, PLUS)
    down_second = send(next_down, MINUS)
    pre = here[0].astype(F32) + got_down[1].astype(F32) + up_second.astype(F32)
    back = here[1].astype(F32) + got_up[1].astype(F32) + down_second.astype(F32)
    return pre, back


def finish(pairs, down, up):
    count = pairs.shape[0]

    def body(pair_ref, down_ref, up_ref, out_ref):
        out_ref[:, :512] = mm(pair_ref[0, 0], down_ref[...], 1, 0).astype(BF16)
        out_ref[:, 512:] = mm(pair_ref[0, 1], up_ref[...], 1, 1).astype(BF16)

    return pl.pallas_call(
        body,
        grid=(count,),
        in_specs=[
            pl.BlockSpec((1, 2, 128, 1024), lambda i: (i, 0, 0, 0)),
            pl.BlockSpec(down.shape, lambda i: (0, 0)),
            pl.BlockSpec(up.shape, lambda i: (0, 0)),
        ],
        out_specs=pl.BlockSpec((128, 1024), lambda i: (i, 0)),
        out_shape=jax.ShapeDtypeStruct((128 * count, 1024), BF16),
        compiler_params=params(),
    )(pairs, down, up)


def all_blocks(share):
    left = send(share, PLUS)
    right = send(share, MINUS)
    left, right = after(left, right)
    left_hidden, right_grad, left, right = after(left[0], right[1], left, right)
    far_hidden = send(left_hidden, PLUS)
    far_grad = send(right_grad, MINUS)
    near = jnp.stack([share, right, left], 0)
    far = jnp.stack([far_hidden, far_grad], 0)[None]
    return near, far, send(near, SIBLING), send(far, SIBLING)


def ordered(near, far):
    return jnp.concatenate([near[:2], far, near[2:]], 0)


def sum_small(block):
    core = lax.axis_index("dp") % 2
    halves = block.reshape(2, 2, 32, 512)
    half = add16(pick(halves, core, 1), send(pick(halves, 1 - core, 1), SIBLING))
    total = half.astype(F32)
    for step in (1, 2, 3):
        total = total + send(half, ring(step)).astype(F32)
    return total


def both_cores(half):
    core = lax.axis_index("dp") % 2
    other = send(half, SIBLING)
    first = jnp.where(core == 0, half, other)
    second = jnp.where(core == 0, other, half)
    return jnp.concatenate([first, second], 1)


def two_parts(block):
    high = block.astype(BF16)
    return high, (block - high.astype(F32)).astype(BF16)


def per_device(tokens, gates, expert_ids, d_mixed, w_up, w_down):
    rows, width = tokens.shape
    groups, near, cap = 32, 16, 32
    up_home = w_up[0]
    down_home = w_down[0]
    me = lax.axis_index("expert")
    at = lax.axis_index("dp")
    quarter, core = at // 2, at % 2
    plane = me // near

    def split(block):
        return block.reshape(near, -1, block.shape[-1])

    def flat(block):
        return block.reshape(-1, block.shape[-1])

    def spread(block):
        return jnp.broadcast_to(block[None], (near,) + block.shape)

    named = expert_ids[:, :, None] == jnp.arange(groups, dtype=jnp.int32)[None, None, :]
    names = jnp.any(named, 1)
    weight = jnp.sum(jnp.where(named, gates[:, :, None], 0.0), 1)
    earlier = jnp.arange(rows)[:, None] > jnp.arange(rows)[None, :]
    place = mm(earlier.astype(BF16), names.astype(BF16), 1, 0).astype(jnp.int32)
    place = jnp.where(names, place, -1)
    hot = jnp.argmax(jnp.sum(names.astype(jnp.int32), 0)).astype(jnp.int32)
    spot = (((place >> 3) - quarter) & 3) * 8 + (place & 7)
    spot = jnp.where((place >= 0) & (place < cap), spot, -1)
    to_send = dispatch(spot.T, weight.T, tokens, d_mixed)
    received = exchange(to_send.reshape(groups, cap, 2 * width))

    hit = spot[:, :, None] == jnp.arange(cap, dtype=jnp.int32)[None, None, :]
    gate_map = jnp.where(hit, weight[:, :, None], 0.0).reshape(rows, groups * cap)
    collect = jnp.concatenate(
        [*two_parts(gate_map), hit.astype(BF16).reshape(rows, groups * cap)], 0
    )
    hit_late = place.T[:, None, :] == jnp.arange(cap, 2 * cap, dtype=jnp.int32)[None, :, None]
    choose_late = jnp.any(hit_late, 0).astype(BF16)
    gate_late = jnp.sum(jnp.where(hit_late, weight.T[:, None, :], 0.0), 0)

    x_late = mm(choose_late, tokens, 1, 0).astype(BF16)
    s_late = mm(choose_late, d_mixed, 1, 0) * jnp.sum(gate_late, 1, keepdims=True)
    hot_send = jnp.concatenate(
        [
            spread(jnp.concatenate([x_late, s_late.astype(BF16)], 0)),
            split(up_home.T),
            split(down_home),
        ],
        1,
    )
    hot_send, received, collect = after(hot_send, received, collect)
    hot_got = exchange_in_plane(hot_send)

    received = received.reshape(2, near, 4, 8, 2 * width)

    def by_quarter(which):
        return pick(received, which).transpose(1, 0, 2, 3).reshape(512, 2 * width)

    own_rows, other_rows = by_quarter(core), by_quarter(1 - core)
    pre, back = sum_over_features(own_rows, other_rows, up_home, down_home)
    hot_got, pre, back = after(hot_got, pre, back)
    logistic = jax.nn.sigmoid(pre)
    share = jnp.stack(
        [pre * logistic, back * logistic * (1.0 + pre * (1.0 - logistic))], 0
    ).astype(BF16)

    x_hot = flat(hot_got[:, :cap])
    s_hot = flat(hot_got[:, cap : 2 * cap])
    slices = pick(hot_got, hot % near)[2 * cap :]
    slices = jnp.where(hot // near == plane, slices, partner(slices))
    up_slice, down_slice = slices[:64], slices[64:]
    parts_hot = jnp.stack([mm(up_slice, x_hot, 1, 1), mm(down_slice, s_hot, 1, 1)], 0)
    sums_hot = sum_small(parts_hot.astype(BF16))
    logistic_hot = jax.nn.sigmoid(sums_hot[0])
    hidden_hot = sums_hot[0] * logistic_hot
    grad_hot = sums_hot[1] * logistic_hot * (1.0 + sums_hot[0] * (1.0 - logistic_hot))
    hidden_hot, grad_hot = both_cores(jnp.stack([hidden_hot, grad_hot], 0).astype(BF16))
    out_hot = mm(hidden_hot, down_slice, 0, 0).astype(BF16)
    in_hot = mm(grad_hot, up_slice, 0, 0).astype(BF16)
    weight_grads = jnp.concatenate(
        [mm(hidden_hot, s_hot, 1, 0), mm(grad_hot, x_hot, 1, 0)], 0
    ).astype(BF16)
    weight_grads = add16(weight_grads, partner(weight_grads))
    share, weight_grads = after(share, weight_grads)
    hot_back = jnp.concatenate([split(out_hot), split(in_hot), spread(weight_grads)], 1)
    hot_home = exchange_in_plane(hot_back)

    pieces = all_blocks(share)
    own_near, own_far, other_near, other_far = [finish(p, down_home, up_home) for p in pieces]

    def by_source(near_rows, far_rows):
        rows_out = jnp.concatenate([near_rows[:256], far_rows, near_rows[256:]], 0)
        return rows_out.reshape(4, near, 8, 2 * width).transpose(1, 0, 2, 3)

    own_out, other_out = by_source(own_near, own_far), by_source(other_near, other_far)
    out_rows = jnp.stack(
        [jnp.where(core == 0, own_out, other_out), jnp.where(core == 0, other_out, own_out)], 0
    )
    out_rows, hot_home, *pieces = after(out_rows, hot_home, *pieces)
    table = flat(exchange(out_rows.reshape(groups, cap, 2 * width)))

    out_late = jnp.sum(hot_home[:, :cap].astype(F32), 0).astype(BF16)
    in_late = jnp.sum(hot_home[:, cap : 2 * cap].astype(F32), 0).astype(BF16)
    is_hot = me == hot
    down_extra = jnp.where(is_hot, flat(hot_home[:, 2 * cap : 2 * cap + 64]), 0)
    up_extra = jnp.where(is_hot, flat(hot_home[:, 2 * cap + 64 :]), 0).T
    units = jnp.concatenate([ordered(pieces[0], pieces[1]), ordered(pieces[2], pieces[3])], 0)
    hidden, grad_pre = units[:, 0].reshape(1024, 1024), units[:, 1].reshape(1024, 1024)
    rows_in = jnp.concatenate([own_rows, other_rows], 0)
    grad_up = mm(rows_in[:, :width], grad_pre, 0, 0) + up_extra.astype(F32)
    grad_down = mm(hidden, rows_in[:, width:], 0, 0) + down_extra.astype(F32)
    high_late, low_late = two_parts(gate_late)
    mixed_late = mm(high_late, out_late, 0, 0) + mm(low_late, out_late, 0, 0)
    tokens_late = mm(choose_late, in_late, 0, 0)

    total = mm(collect, table, 1, 0)
    mixed = total[:rows, :width] + total[rows : 2 * rows, :width] + mixed_late
    d_tokens = total[2 * rows :, width:] + tokens_late
    return (
        mixed.astype(BF16),
        d_tokens.astype(BF16),
        grad_up.astype(BF16)[None],
        grad_down.astype(BF16)[None],
    )


def solution(mesh):
    in_specs = (
        P("expert", "dp"),
        P("expert", None),
        P("expert", None),
        P("expert", "dp"),
        P("expert", "dp", None),
        P("expert", None, "dp"),
    )
    out_specs = (
        P("expert", "dp"),
        P("expert", "dp"),
        P("expert", "dp", None),
        P("expert", None, "dp"),
    )
    return jax.shard_map(
        per_device, mesh=mesh, in_specs=in_specs, out_specs=out_specs, check_vma=False
    )
```

profile of v0, /device:TPU:2, one launch (start us, length us, event | category | flops | bytes accessed | tf_op | source)
XLA Modules:
  0.0 238.4 jit_solution(15523021462628218061)
XLA Ops:
  6.7 9.2 %all-to-all-start = ((bf16[32,32,1024]{2,1,0:T(8,128)(2,1)}), bf16[32,32,1024]{2,1,0:T(8,128)(2,1)}, u32[]{:S(2)}, u32[]{:S(2)}) async-start(bf16[32,32,1024]{2,1,0:T(8,128)(2,1)} %bitcast.164), calls=%async_computation | async-start | bytes 4194304 | tf_op jit(solution)/shard_map/all_to_all | solution.py:28
  24.1 19.3 %all-to-all-done = bf16[32,32,1024]{2,1,0:T(8,128)(2,1)} async-done(((bf16[32,32,1024]{2,1,0:T(8,128)(2,1)}), bf16[32,32,1024]{2,1,0:T(8,128)(2,1)}, u32[]{:S(2)}, u32[]{:S(2)}) %all-to-all-start) | async-done | bytes 2097184 | tf_op jit(solution)/shard_map/all_to_all | solution.py:28
  45.3 2.6 %shard_map.94 = bf16[8,128,1024]{2,1,0:T(8,128)(2,1)} custom-call(bf16[512,1024]{1,0:T(8,128)(2,1)S(1)} %bitcast.165, bf16[512,1024]{1,0:T(8,128)(2,1)S(1)} %bitcast.158, bf16[1024,512]{1,0:T(8,128)(2,1)S(1)} %bitcast.151), custom_call_target="tpu_custom_call" | custom-call | tf_op jit(solution)/shard_map/pallas_call | solution.py:98
  47.9 5.6 %all-to-all-start.1 = ((bf16[16,192,512]{2,1,0:T(8,128)(2,1)}), bf16[16,192,512]{2,1,0:T(8,128)(2,1)}, u32[]{:S(2)}, u32[]{:S(2)}) async-start(bf16[16,192,512]{2,1,0:T(8,128)(2,1)} %pad_maximum_fusion), calls=%async_computation.1 | async-start | bytes 6291456 | tf_op jit(solution)/shard_map/all_to_all | solution.py:32
  53.6 3.2 %shard_map.95 = (bf16[2,128,1024]{2,1,0:T(8,128)(2,1)S(1)}, bf16[2,128,1024]{2,1,0:T(8,128)(2,1)S(1)}, bf16[2,128,1024]{2,1,0:T(8,128)(2,1)S(1)}, bf16[2,128,1024]{2,1,0:T(8,128)(2,1)S(1)}) custom-call(bf16[512,1024]{1,0:T(8,128)(2,1)S(1)} %bitcast.168, bf16[512,1024]{1,0:T(8,128)(2,1)S(1)} %bitcast.159, bf16[1024,512]{1,0:T(8,128)(2,1)S(1)} %bitcast.152, ...), custom_call_target="tpu_custom_call" | custom-call | tf_op jit(solution)/shard_map/pallas_call | solution.py:115
  56.8 3.4 %collective-permute-start.1 = (bf16[2,128,1024]{2,1,0:T(8,128)(2,1)S(1)}, bf16[2,128,1024]{2,1,0:T(8,128)(2,1)S(1)}, u32[]{:S(2)}, u32[]{:S(2)}) collective-permute-start(bf16[2,128,1024]{2,1,0:T(8,128)(2,1)S(1)} %get-tuple-element.40), channel_id=1, source_target_pairs={{0,64},{32,96},{64,128},{96,160},{128,192},{160,224},{192,0},{224,... | collective-permute-start | bytes 1572872 | tf_op jit(solution)/shard_map/ppermute | solution.py:42
  62.4 12.4 %collective-permute-done.1 = bf16[2,128,1024]{2,1,0:T(8,128)(2,1)S(1)} collective-permute-done((bf16[2,128,1024]{2,1,0:T(8,128)(2,1)S(1)}, bf16[2,128,1024]{2,1,0:T(8,128)(2,1)S(1)}, u32[]{:S(2)}, u32[]{:S(2)}) %collective-permute-start.1) | collective-permute-done | bytes 524320 | tf_op jit(solution)/shard_map/ppermute | solution.py:42
  74.8 10.4 %collective-permute-done.2 = bf16[2,128,1024]{2,1,0:T(8,128)(2,1)S(1)} collective-permute-done((bf16[2,128,1024]{2,1,0:T(8,128)(2,1)S(1)}, bf16[2,128,1024]{2,1,0:T(8,128)(2,1)S(1)}, u32[]{:S(2)}, u32[]{:S(2)}) %collective-permute-start.2) | collective-permute-done | bytes 524320 | tf_op jit(solution)/shard_map/ppermute | solution.py:42
  86.3 5.7 %collective-permute-start.3 = (bf16[128,1024]{1,0:T(8,128)(2,1)}, bf16[128,1024]{1,0:T(8,128)(2,1)S(1)}, u32[]{:S(2)}, u32[]{:S(2)}) collective-permute-start(bf16[128,1024]{1,0:T(8,128)(2,1)} %get-tuple-element.47), channel_id=1, source_target_pairs={{0,64},{32,96},{64,128},{96,160},{128,192},{160,224},{192,0},{224,... | collective-permute-start | bytes 786440 | tf_op jit(solution)/shard_map/ppermute | solution.py:42
  95.4 6.4 %collective-permute-done.3 = bf16[128,1024]{1,0:T(8,128)(2,1)S(1)} collective-permute-done((bf16[128,1024]{1,0:T(8,128)(2,1)}, bf16[128,1024]{1,0:T(8,128)(2,1)S(1)}, u32[]{:S(2)}, u32[]{:S(2)}) %collective-permute-start.3) | collective-permute-done | bytes 262176 | tf_op jit(solution)/shard_map/ppermute | solution.py:42
  101.8 2.3 bitcast_add_fusion.1
  105.0 4.1 %collective-permute-start.5 = (bf16[128,512]{1,0:T(8,128)(2,1)S(1)}, bf16[128,512]{1,0:T(8,128)(2,1)S(1)}, u32[]{:S(2)}, u32[]{:S(2)}) collective-permute-start(bf16[128,512]{1,0:T(8,128)(2,1)S(1)} %dynamic-slice_bitcast_fusion), channel_id=1, source_target_pairs={{0,16},{1,17},{2,18},{3,19},{4,20},{5,21},{6,22},{7,23},{8,24},{9,... | collective-permute-start | bytes 393224 | tf_op jit(solution)/shard_map/ppermute | solution.py:38
  118.6 4.9 %collective-permute-start.8 = (bf16[2,32,512]{2,1,0:T(8,128)(2,1)S(1)}, bf16[2,32,512]{2,1,0:T(8,128)(2,1)S(1)}, u32[]{:S(2)}, u32[]{:S(2)}) collective-permute-start(bf16[2,32,512]{2,1,0:T(8,128)(2,1)S(1)} %fusion.22), channel_id=1, source_target_pairs={{0,128},{32,160},{64,192},{96,224},{128,0},{160,32},{192,64},{224,... | collective-permute-start | bytes 196616 | tf_op jit(solution)/shard_map/ppermute | solution.py:42
  124.9 4.2 %collective-permute-done.8 = bf16[2,32,512]{2,1,0:T(8,128)(2,1)S(1)} collective-permute-done((bf16[2,32,512]{2,1,0:T(8,128)(2,1)S(1)}, bf16[2,32,512]{2,1,0:T(8,128)(2,1)S(1)}, u32[]{:S(2)}, u32[]{:S(2)}) %collective-permute-start.8) | collective-permute-done | bytes 65568 | tf_op jit(solution)/shard_map/ppermute | solution.py:42
  134.3 4.5 %collective-permute-done.11 = bf16[128,512]{1,0:T(8,128)(2,1)S(1)} collective-permute-done((bf16[128,512]{1,0:T(8,128)(2,1)S(1)}, bf16[128,512]{1,0:T(8,128)(2,1)S(1)}, u32[]{:S(2)}, u32[]{:S(2)}) %collective-permute-start.11) | collective-permute-done | bytes 131104 | tf_op jit(solution)/shard_map/ppermute | solution.py:38
  140.8 4.9 %all-to-all-start.2 = ((bf16[16,192,512]{2,1,0:T(8,128)(2,1)}), bf16[16,192,512]{2,1,0:T(8,128)(2,1)}, u32[]{:S(2)}, u32[]{:S(2)}) async-start(bf16[16,192,512]{2,1,0:T(8,128)(2,1)} %pad_maximum_fusion.1), calls=%async_computation.2 | async-start | bytes 6291456 | tf_op jit(solution)/shard_map/all_to_all | solution.py:32
  148.7 18.1 %collective-permute-done.13 = bf16[2,128,1024]{2,1,0:T(8,128)(2,1)S(1)} collective-permute-done((bf16[2,128,1024]{2,1,0:T(8,128)(2,1)S(1)}, bf16[2,128,1024]{2,1,0:T(8,128)(2,1)S(1)}, u32[]{:S(2)}, u32[]{:S(2)}) %collective-permute-start.13) | collective-permute-done | bytes 524320 | tf_op jit(solution)/shard_map/ppermute | solution.py:42
  171.3 7.7 %collective-permute-done.14 = bf16[128,1024]{1,0:T(8,128)(2,1)S(1)} collective-permute-done((bf16[128,1024]{1,0:T(8,128)(2,1)S(1)}, bf16[128,1024]{1,0:T(8,128)(2,1)S(1)}, u32[]{:S(2)}, u32[]{:S(2)}) %collective-permute-start.14) | collective-permute-done | bytes 262176 | tf_op jit(solution)/shard_map/ppermute | solution.py:42
  179.0 10.7 %collective-permute-done.15 = bf16[128,1024]{1,0:T(8,128)(2,1)S(1)} collective-permute-done((bf16[128,1024]{1,0:T(8,128)(2,1)S(1)}, bf16[128,1024]{1,0:T(8,128)(2,1)S(1)}, u32[]{:S(2)}, u32[]{:S(2)}) %collective-permute-start.15) | collective-permute-done | bytes 262176 | tf_op jit(solution)/shard_map/ppermute | solution.py:42
  198.0 7.4 %all-to-all-start.3 = ((bf16[32,32,1024]{2,1,0:T(8,128)(2,1)}), bf16[32,32,1024]{2,1,0:T(8,128)(2,1)}, u32[]{:S(2)}, u32[]{:S(2)}) async-start(bf16[32,32,1024]{2,1,0:T(8,128)(2,1)} %bitcast.54), calls=%async_computation.3 | async-start | bytes 4194304 | tf_op jit(solution)/shard_map/all_to_all | solution.py:28
  206.0 2.7 %slice_select_fusion = (bf16[16,64,512]{2,1,0:T(8,128)(2,1)}, bf16[16,64,512]{2,1,0:T(8,128)(2,1)S(1)}) fusion(bf16[16,192,512]{2,1,0:T(8,128)(2,1)} %all-to-all-done.2, pred[]{:T(512)S(6)} %eq.80), kind=kLoop, calls=%fused_computation.38 | loop fusion | flops 1048576 | bytes 4194305 | tf_op jit(solution)/shard_map/jit(_where)/select_n | solution.py:300
  210.4 3.0 %copy.39 = f32[1024,512]{0,1:T(8,128)} copy(f32[1024,512]{1,0:T(8,128)} %bitcast_convert_fusion) | data formatting | bytes 4194304 | tf_op jit(solution)/shard_map/convert_element_type | solution.py:305
  223.0 11.1 %all-to-all-done.3 = bf16[32,32,1024]{2,1,0:T(8,128)(2,1)} async-done(((bf16[32,32,1024]{2,1,0:T(8,128)(2,1)}), bf16[32,32,1024]{2,1,0:T(8,128)(2,1)}, u32[]{:S(2)}, u32[]{:S(2)}) %all-to-all-start.3) | async-done | bytes 2097184 | tf_op jit(solution)/shard_map/all_to_all | solution.py:28
  234.1 2.6 %fusion.49 = f32[384,1024]{1,0:T(8,128)S(1)} fusion(bf16[384,1024]{0,1:T(8,128)(2,1)S(1)} %copy-done.16, bf16[1024,1024]{1,0:T(8,128)(2,1)} %bitcast.55), kind=kOutput, calls=%fused_computation.130 | convolution fusion | flops 805306368 | bytes 4456448 | tf_op jit(solution)/shard_map/dot_general | solution.py:24
  (147 shorter events, 67.4 us)
Async XLA Ops:
  6.7 36.7 %all-to-all-start = ((bf16[32,32,1024]{2,1,0:T(8,128)(2,1)}), bf16[32,32,1024]{2,1,0:T(8,128)(2,1)}, u32[]{:S(2)}, u32[]{:S(2)}) async-start(bf16[32,32,1024]{2,1,0:T(8,128)(2,1)} %bitcast.164), calls=%async_computation | async-start | bytes 4194304 | tf_op jit(solution)/shard_map/all_to_all | solution.py:28
  47.9 5.7 %collective-permute-start = (bf16[8,128,1024]{2,1,0:T(8,128)(2,1)}, bf16[8,128,1024]{2,1,0:T(8,128)(2,1)}, u32[]{:S(2)}, u32[]{:S(2)}) collective-permute-start(bf16[8,128,1024]{2,1,0:T(8,128)(2,1)} %shard_map.94), channel_id=1, source_target_pairs={{0,32},{32,0},{64,96},{96,64},{128,160},{160,128},{192,224},{224,1... | collective-permute-start | bytes 6291464 | tf_op jit(solution)/shard_map/ppermute | solution.py:42
  47.9 56.2 %all-to-all-start.1 = ((bf16[16,192,512]{2,1,0:T(8,128)(2,1)}), bf16[16,192,512]{2,1,0:T(8,128)(2,1)}, u32[]{:S(2)}, u32[]{:S(2)}) async-start(bf16[16,192,512]{2,1,0:T(8,128)(2,1)} %pad_maximum_fusion), calls=%async_computation.1 | async-start | bytes 6291456 | tf_op jit(solution)/shard_map/all_to_all | solution.py:32
  56.8 18.0 %collective-permute-start.1 = (bf16[2,128,1024]{2,1,0:T(8,128)(2,1)S(1)}, bf16[2,128,1024]{2,1,0:T(8,128)(2,1)S(1)}, u32[]{:S(2)}, u32[]{:S(2)}) collective-permute-start(bf16[2,128,1024]{2,1,0:T(8,128)(2,1)S(1)} %get-tuple-element.40), channel_id=1, source_target_pairs={{0,64},{32,96},{64,128},{96,160},{128,192},{160,224},{192,0},{224,... | collective-permute-start | bytes 1572872 | tf_op jit(solution)/shard_map/ppermute | solution.py:42
  60.2 25.1 %collective-permute-start.2 = (bf16[2,128,1024]{2,1,0:T(8,128)(2,1)S(1)}, bf16[2,128,1024]{2,1,0:T(8,128)(2,1)S(1)}, u32[]{:S(2)}, u32[]{:S(2)}) collective-permute-start(bf16[2,128,1024]{2,1,0:T(8,128)(2,1)S(1)} %get-tuple-element.41), channel_id=1, source_target_pairs={{0,192},{32,224},{64,0},{96,32},{128,64},{160,96},{192,128},{224,1... | collective-permute-start | bytes 1572872 | tf_op jit(solution)/shard_map/ppermute | solution.py:42
  86.3 15.5 %collective-permute-start.3 = (bf16[128,1024]{1,0:T(8,128)(2,1)}, bf16[128,1024]{1,0:T(8,128)(2,1)S(1)}, u32[]{:S(2)}, u32[]{:S(2)}) collective-permute-start(bf16[128,1024]{1,0:T(8,128)(2,1)} %get-tuple-element.47), channel_id=1, source_target_pairs={{0,64},{32,96},{64,128},{96,160},{128,192},{160,224},{192,0},{224,... | collective-permute-start | bytes 786440 | tf_op jit(solution)/shard_map/ppermute | solution.py:42
  92.0 9.8 %collective-permute-start.4 = (bf16[128,1024]{1,0:T(8,128)(2,1)}, bf16[128,1024]{1,0:T(8,128)(2,1)}, u32[]{:S(2)}, u32[]{:S(2)}) collective-permute-start(bf16[128,1024]{1,0:T(8,128)(2,1)} %get-tuple-element.49), channel_id=1, source_target_pairs={{0,192},{32,224},{64,0},{96,32},{128,64},{160,96},{192,128},{224,1... | collective-permute-start | bytes 786440 | tf_op jit(solution)/shard_map/ppermute | solution.py:42
  105.0 7.5 %collective-permute-start.5 = (bf16[128,512]{1,0:T(8,128)(2,1)S(1)}, bf16[128,512]{1,0:T(8,128)(2,1)S(1)}, u32[]{:S(2)}, u32[]{:S(2)}) collective-permute-start(bf16[128,512]{1,0:T(8,128)(2,1)S(1)} %dynamic-slice_bitcast_fusion), channel_id=1, source_target_pairs={{0,16},{1,17},{2,18},{3,19},{4,20},{5,21},{6,22},{7,23},{8,24},{9,... | collective-permute-start | bytes 393224 | tf_op jit(solution)/shard_map/ppermute | solution.py:38
  114.1 1.5 collective-permute-start.6
  116.4 8.4 %collective-permute-start.9 = (bf16[2,32,512]{2,1,0:T(8,128)(2,1)S(1)}, bf16[2,32,512]{2,1,0:T(8,128)(2,1)S(1)}, u32[]{:S(2)}, u32[]{:S(2)}) collective-permute-start(bf16[2,32,512]{2,1,0:T(8,128)(2,1)S(1)} %fusion.22), channel_id=1, source_target_pairs={{0,192},{32,224},{64,0},{96,32},{128,64},{160,96},{192,128},{224,1... | collective-permute-start | bytes 196616 | tf_op jit(solution)/shard_map/ppermute | solution.py:42
  118.6 10.5 %collective-permute-start.8 = (bf16[2,32,512]{2,1,0:T(8,128)(2,1)S(1)}, bf16[2,32,512]{2,1,0:T(8,128)(2,1)S(1)}, u32[]{:S(2)}, u32[]{:S(2)}) collective-permute-start(bf16[2,32,512]{2,1,0:T(8,128)(2,1)S(1)} %fusion.22), channel_id=1, source_target_pairs={{0,128},{32,160},{64,192},{96,224},{128,0},{160,32},{192,64},{224,... | collective-permute-start | bytes 196616 | tf_op jit(solution)/shard_map/ppermute | solution.py:42
  123.4 7.4 %collective-permute-start.7 = (bf16[2,32,512]{2,1,0:T(8,128)(2,1)S(1)}, bf16[2,32,512]{2,1,0:T(8,128)(2,1)S(1)}, u32[]{:S(2)}, u32[]{:S(2)}) collective-permute-start(bf16[2,32,512]{2,1,0:T(8,128)(2,1)S(1)} %fusion.22), channel_id=1, source_target_pairs={{0,64},{32,96},{64,128},{96,160},{128,192},{160,224},{192,0},{224,... | collective-permute-start | bytes 196616 | tf_op jit(solution)/shard_map/ppermute | solution.py:42
  131.0 1.3 collective-permute-start.10
  133.1 5.6 %collective-permute-start.11 = (bf16[128,512]{1,0:T(8,128)(2,1)S(1)}, bf16[128,512]{1,0:T(8,128)(2,1)S(1)}, u32[]{:S(2)}, u32[]{:S(2)}) collective-permute-start(bf16[128,512]{1,0:T(8,128)(2,1)S(1)} %pad_maximum_fusion.10), channel_id=1, source_target_pairs={{0,16},{1,17},{2,18},{3,19},{4,20},{5,21},{6,22},{7,23},{8,24},{9,... | collective-permute-start | bytes 393224 | tf_op jit(solution)/shard_map/ppermute | solution.py:38
  140.8 57.1 %all-to-all-start.2 = ((bf16[16,192,512]{2,1,0:T(8,128)(2,1)}), bf16[16,192,512]{2,1,0:T(8,128)(2,1)}, u32[]{:S(2)}, u32[]{:S(2)}) async-start(bf16[16,192,512]{2,1,0:T(8,128)(2,1)} %pad_maximum_fusion.1), calls=%async_computation.2 | async-start | bytes 6291456 | tf_op jit(solution)/shard_map/all_to_all | solution.py:32
  145.7 21.1 %collective-permute-start.13 = (bf16[2,128,1024]{2,1,0:T(8,128)(2,1)S(1)}, bf16[2,128,1024]{2,1,0:T(8,128)(2,1)S(1)}, u32[]{:S(2)}, u32[]{:S(2)}) collective-permute-start(bf16[2,128,1024]{2,1,0:T(8,128)(2,1)S(1)} %copy-done.18), channel_id=1, source_target_pairs={{0,192},{32,224},{64,0},{96,32},{128,64},{160,96},{192,128},{224,1... | collective-permute-start | bytes 1572872 | tf_op jit(solution)/shard_map/ppermute | solution.py:42
  146.7 20.1 %collective-permute-start.12 = (bf16[2,128,1024]{2,1,0:T(8,128)(2,1)S(1)}, bf16[2,128,1024]{2,1,0:T(8,128)(2,1)S(1)}, u32[]{:S(2)}, u32[]{:S(2)}) collective-permute-start(bf16[2,128,1024]{2,1,0:T(8,128)(2,1)S(1)} %copy-done.18), channel_id=1, source_target_pairs={{0,64},{32,96},{64,128},{96,160},{128,192},{160,224},{192,0},{224,... | collective-permute-start | bytes 1572872 | tf_op jit(solution)/shard_map/ppermute | solution.py:42
  167.0 24.9 %copy-start.2 = (bf16[3,2,128,1024]{3,2,1,0:T(8,128)(2,1)}, bf16[3,2,128,1024]{3,2,1,0:T(8,128)(2,1)S(1)}, u32[]{:S(2)}) copy-start(bf16[3,2,128,1024]{3,2,1,0:T(8,128)(2,1)S(1)} %pad_maximum_fusion.3.pair_ref) | copy-start | bytes 4718596
  167.0 26.5 %collective-permute-start.16 = (bf16[3,2,128,1024]{3,2,1,0:T(8,128)(2,1)S(1)}, bf16[3,2,128,1024]{3,2,1,0:T(8,128)(2,1)S(1)}, u32[]{:S(2)}, u32[]{:S(2)}) collective-permute-start(bf16[3,2,128,1024]{3,2,1,0:T(8,128)(2,1)S(1)} %pad_maximum_fusion.3.pair_ref), channel_id=1, source_target_pairs={{0,32},{32,0},{64,96},{96,64},{128,160},{160,128},{192,224},{224,1... | collective-permute-start | bytes 4718600 | tf_op jit(solution)/shard_map/ppermute | solution.py:42
  167.1 11.9 %collective-permute-start.14 = (bf16[128,1024]{1,0:T(8,128)(2,1)S(1)}, bf16[128,1024]{1,0:T(8,128)(2,1)S(1)}, u32[]{:S(2)}, u32[]{:S(2)}) collective-permute-start(bf16[128,1024]{1,0:T(8,128)(2,1)S(1)} %get-tuple-element.59), channel_id=1, source_target_pairs={{0,64},{32,96},{64,128},{96,160},{128,192},{160,224},{192,0},{224,... | collective-permute-start | bytes 786440 | tf_op jit(solution)/shard_map/ppermute | solution.py:42
  169.4 20.3 %collective-permute-start.15 = (bf16[128,1024]{1,0:T(8,128)(2,1)S(1)}, bf16[128,1024]{1,0:T(8,128)(2,1)S(1)}, u32[]{:S(2)}, u32[]{:S(2)}) collective-permute-start(bf16[128,1024]{1,0:T(8,128)(2,1)S(1)} %get-tuple-element.60), channel_id=1, source_target_pairs={{0,192},{32,224},{64,0},{96,32},{128,64},{160,96},{192,128},{224,1... | collective-permute-start | bytes 786440 | tf_op jit(solution)/shard_map/ppermute | solution.py:42
  189.8 3.0 %collective-permute-start.17 = (bf16[1,2,128,1024]{3,2,1,0:T(8,128)(2,1)S(1)}, bf16[1,2,128,1024]{3,2,1,0:T(8,128)(2,1)S(1)}, u32[]{:S(2)}, u32[]{:S(2)}) collective-permute-start(bf16[1,2,128,1024]{3,2,1,0:T(8,128)(2,1)S(1)} %maximum_bitcast_fusion.pair_ref), channel_id=1, source_target_pairs={{0,32},{32,0},{64,96},{96,64},{128,160},{160,128},{192,224},{224,1... | collective-permute-start | bytes 1572872 | tf_op jit(solution)/shard_map/ppermute | solution.py:42
  198.0 36.1 %all-to-all-start.3 = ((bf16[32,32,1024]{2,1,0:T(8,128)(2,1)}), bf16[32,32,1024]{2,1,0:T(8,128)(2,1)}, u32[]{:S(2)}, u32[]{:S(2)}) async-start(bf16[32,32,1024]{2,1,0:T(8,128)(2,1)} %bitcast.54), calls=%async_computation.3 | async-start | bytes 4194304 | tf_op jit(solution)/shard_map/all_to_all | solution.py:28
  220.7 13.4 %copy-start.16 = (bf16[384,1024]{0,1:T(8,128)(2,1)S(1)}, bf16[384,1024]{0,1:T(8,128)(2,1)}, u32[]{:S(2)}) copy-start(bf16[384,1024]{0,1:T(8,128)(2,1)} %pad_maximum_fusion.8) | copy-start | bytes 2359300
  (21 other events, 56.2 us)
where the time goes:
time: 240 us; the launch traced here: 238 us
  waiting for transfers between devices  111 us (46%)
  starting transfers between devices  57.9 us (24%)
  other arithmetic  26.9 us (11%)
  local copies, waits for them, and re-layouts  15.2 us (6%)
  Pallas kernels  12.3 us (5%)
  matrix products  11.1 us (5%)
  between operations  4.61 us (2%)
    ppermute x16, waiting for transfers between devices, send(): return lax.ppermute(block, 'dp', pairs)  73.6 us
    all_to_all x2, waiting for transfers between devices, exchange(): lax.all_to_all(payload, 'expert', split_axis=0, concat_axis=0, tiled=True)  30.4 us
    ppermute x16, starting transfers between devices, send(): return lax.ppermute(block, 'dp', pairs)  25.9 us
    all_to_all x2, starting transfers between devices, exchange(): lax.all_to_all(payload, 'expert', split_axis=0, concat_axis=0, tiled=True)  16.6 us
    dot_general x15, matrix products, mm(): return lax.dot_general(left, right, dims, preferred_element_type=F32)  11.1 us
    all_to_all x2, starting transfers between devices, exchange_in_plane(): lax.all_to_all(payload, 'expert', split_axis=0, concat_axis=0, tiled=True...  10.4 us
    ppermute x2, waiting for transfers between devices, partner(): return lax.ppermute(block, 'expert', PARTNER)  6.55 us
    unnamed x49, local copies, waits for them, and re-layouts  6.38 us
  transfers between devices with their start and end apart: 22, of which 14 were waited for; matrix products, arithmetic and copies ran while one was open for 14% of the time, Pallas kernels for 4%

commit v1 on v0

--- a/solution.py
+++ b/solution.py
@@ -83,7 +83,7 @@
     )(spot[:, None], gate[:, None], tokens, mixed)
 
 
-ORDER = ((0, 2), (1, 1), (1, 2), (0, 3), (0, 1), (1, 3), (0, 0), (1, 0))
+ORDER = ((0, 2), (1, 2), (1, 1), (0, 3), (0, 1), (1, 3), (0, 0), (1, 0))
 
 
 def parts_for_sibling(rows, up, down):
@@ -110,27 +110,27 @@
         )
         for i, (which, block) in enumerate(ORDER):
             part = product[which][128 * block : 128 * block + 128]
-            out_refs[i // 2][i % 2] = (part + came_ref[i].astype(F32)).astype(BF16)
+            out_refs[i][...] = (part + came_ref[i].astype(F32)).astype(BF16)
 
     return pl.pallas_call(
         body,
-        out_shape=[jax.ShapeDtypeStruct((2, 128, 1024), BF16)] * 4,
+        out_shape=[jax.ShapeDtypeStruct((128, 1024), BF16)] * 8,
         compiler_params=params(),
     )(rows, up, down, came)
 
 
 def sum_over_features(own, other, up, down):
     came = send(parts_for_sibling(other, up, down), SIBLING)
-    first_up, first_down, second, here = parts_with_sibling(own, up, down, came)
-    got_up, got_down = after(send(first_up, PLUS), send(first_down, MINUS))
-    next_up, next_down, got_up, got_down, here = after(
-        add16(second[0], got_up[0]), add16(second[1], got_down[0]), got_up, got_down, here
-    )
+    parts = parts_with_sibling(own, up, down, came)
+    far_up, far_down, near_back, near_pre, next_up, next_down, here_pre, here_back = parts
+    got_up, got_down = after(send(far_up, PLUS), send(far_down, MINUS))
+    near_back, near_pre = send(near_back, PLUS), send(near_pre, MINUS)
+    next_up, next_down = after(add16(next_up, got_up), add16(next_down, got_down))
     up_second = send(next_up, PLUS)
     down_second = send(next_down, MINUS)
-    pre = here[0].astype(F32) + got_down[1].astype(F32) + up_second.astype(F32)
-    back = here[1].astype(F32) + got_up[1].astype(F32) + down_second.astype(F32)
-    return pre, back
+    pre = here_pre.astype(F32) + near_pre.astype(F32) + up_second.astype(F32)
+    back = here_back.astype(F32) + near_back.astype(F32) + down_second.astype(F32)
+    return pre, back, next_up, next_down
 
 
 def finish(pairs, down, up):
@@ -154,26 +154,36 @@
     )(pairs, down, up)
 
 
-def all_blocks(share):
+def all_blocks(share, hot_back, use):
     left = send(share, PLUS)
     right = send(share, MINUS)
+    other_share = send(share, SIBLING)
+    hot_back, other_share = after(hot_back, other_share)
     left, right = after(left, right)
     left_hidden, right_grad, left, right = after(left[0], right[1], left, right)
     far_hidden = send(left_hidden, PLUS)
     far_grad = send(right_grad, MINUS)
-    near = jnp.stack([share, right, left], 0)
+    sides = jnp.stack([right, left], 0)
+    other_sides = send(sides, SIBLING)
+    near = jnp.concatenate([share[None], sides], 0)
+    other_near = jnp.concatenate([other_share[None], other_sides], 0)
+    used_near, used_other = use(near), use(other_near)
+    far_hidden, far_grad, used_near, used_other = after(far_hidden, far_grad, used_near, used_other)
     far = jnp.stack([far_hidden, far_grad], 0)[None]
-    return near, far, send(near, SIBLING), send(far, SIBLING)
+    other_far = send(far, SIBLING)
+    used = used_near, use(far), used_other, use(other_far)
+    return (near, far, other_near, other_far), used, hot_back
 
 
 def ordered(near, far):
     return jnp.concatenate([near[:2], far, near[2:]], 0)
 
 
-def sum_small(block):
+def sum_small(block, *earlier):
     core = lax.axis_index("dp") % 2
     halves = block.reshape(2, 2, 32, 512)
     half = add16(pick(halves, core, 1), send(pick(halves, 1 - core, 1), SIBLING))
+    half = after(half, *earlier)[0]
     total = half.astype(F32)
     for step in (1, 2, 3):
         total = total + send(half, ring(step)).astype(F32)
@@ -252,8 +262,8 @@
         return pick(received, which).transpose(1, 0, 2, 3).reshape(512, 2 * width)
 
     own_rows, other_rows = by_quarter(core), by_quarter(1 - core)
-    pre, back = sum_over_features(own_rows, other_rows, up_home, down_home)
-    hot_got, pre, back = after(hot_got, pre, back)
+    pre, back, *started = sum_over_features(own_rows, other_rows, up_home, down_home)
+    hot_got = after(hot_got, *started)[0]
     logistic = jax.nn.sigmoid(pre)
     share = jnp.stack(
         [pre * logistic, back * logistic * (1.0 + pre * (1.0 - logistic))], 0
@@ -265,7 +275,7 @@
     slices = jnp.where(hot // near == plane, slices, partner(slices))
     up_slice, down_slice = slices[:64], slices[64:]
     parts_hot = jnp.stack([mm(up_slice, x_hot, 1, 1), mm(down_slice, s_hot, 1, 1)], 0)
-    sums_hot = sum_small(parts_hot.astype(BF16))
+    sums_hot = sum_small(parts_hot.astype(BF16), pre, back)
     logistic_hot = jax.nn.sigmoid(sums_hot[0])
     hidden_hot = sums_hot[0] * logistic_hot
     grad_hot = sums_hot[1] * logistic_hot * (1.0 + sums_hot[0] * (1.0 - logistic_hot))
@@ -278,10 +288,11 @@
     weight_grads = add16(weight_grads, partner(weight_grads))
     share, weight_grads = after(share, weight_grads)
     hot_back = jnp.concatenate([split(out_hot), split(in_hot), spread(weight_grads)], 1)
+    pieces, used, hot_back = all_blocks(
+        share, hot_back, lambda pairs: finish(pairs, down_home, up_home)
+    )
     hot_home = exchange_in_plane(hot_back)
-
-    pieces = all_blocks(share)
-    own_near, own_far, other_near, other_far = [finish(p, down_home, up_home) for p in pieces]
+    own_near, own_far, other_near, other_far = used
 
     def by_source(near_rows, far_rows):
         rows_out = jnp.concatenate([near_rows[:256], far_rows, near_rows[256:]], 0)

time: 240 us -> 232 us (0.967)
  waiting for transfers between devices: 111 us -> 83.8 us
  starting transfers between devices: 57.9 us -> 74.6 us
    ppermute x16 -> x19, waiting for transfers between devices: 73.6 us -> 27.7 us  [send(): return lax.ppermute(block, 'dp', pairs)]
    all_to_all x2, waiting for transfers between devices: 0.01 us -> 22.3 us  [exchange_in_plane(): lax.all_to_all(payload, 'expert', split_axis=0, concat_axis=0, tiled=True...]
    ppermute x16 -> x19, starting transfers between devices: 25.9 us -> 34.1 us  [send(): return lax.ppermute(block, 'dp', pairs)]
    all_to_all x2, starting transfers between devices: 10.4 us -> 15.9 us  [exchange_in_plane(): lax.all_to_all(payload, 'expert', split_axis=0, concat_axis=0, tiled=True...]
    concatenate x0 -> x2, other arithmetic: none -> 2.68 us  [the longest x1 1.46 us: all_blocks(): other_near = jnp.concatenate([other_share[None], other_sides], 0)]
    unnamed x49 -> x57, local copies, waits for them, and re-layouts: 6.38 us -> 6.21 us
  transfers between devices with their start and end apart: 22 -> 25, of which waited for: 14 -> 13; matrix products, arithmetic and copies ran while one was open for 14% -> 17% of each run, Pallas kernels for 4% -> 4%
where the time goes in v1:
time: 232 us; the launch traced here: 231 us
  waiting for transfers between devices  83.8 us (36%)
  starting transfers between devices  74.6 us (32%)
  other arithmetic  28.2 us (12%)
  local copies, waits for them, and re-layouts  15 us (6%)
  Pallas kernels  12.3 us (5%)
  matrix products  12.1 us (5%)
  between operations  4.68 us (2%)
    ppermute x19, starting transfers between devices, send(): return lax.ppermute(block, 'dp', pairs)  34.1 us
    all_to_all x2, waiting for transfers between devices, exchange(): lax.all_to_all(payload, 'expert', split_axis=0, concat_axis=0, tiled=True)  28.6 us
    ppermute x19, waiting for transfers between devices, send(): return lax.ppermute(block, 'dp', pairs)  27.7 us
    all_to_all x2, waiting for transfers between devices, exchange_in_plane(): lax.all_to_all(payload, 'expert', split_axis=0, concat_axis=0, tiled=True...  22.3 us
    all_to_all x2, starting transfers between devices, exchange(): lax.all_to_all(payload, 'expert', split_axis=0, concat_axis=0, tiled=True)  18.9 us
    all_to_all x2, starting transfers between devices, exchange_in_plane(): lax.all_to_all(payload, 'expert', split_axis=0, concat_axis=0, tiled=True...  15.9 us
    dot_general x15, matrix products, mm(): return lax.dot_general(left, right, dims, preferred_element_type=F32)  12.1 us
    unnamed x57, local copies, waits for them, and re-layouts  6.21 us
  transfers between devices with their start and end apart: 25, of which 13 were waited for; matrix products, arithmetic and copies ran while one was open for 17% of the time, Pallas kernels for 4%

profile of v1, /device:TPU:2, one launch (start us, length us, event | category | flops | bytes accessed | tf_op | source)
XLA Modules:
  0.0 230.6 jit_solution(17273929695586070172)
XLA Ops:
  6.7 9.2 %all-to-all-start = ((bf16[32,32,1024]{2,1,0:T(8,128)(2,1)}), bf16[32,32,1024]{2,1,0:T(8,128)(2,1)}, u32[]{:S(2)}, u32[]{:S(2)}) async-start(bf16[32,32,1024]{2,1,0:T(8,128)(2,1)} %bitcast.157), calls=%async_computation | async-start | bytes 4194304 | tf_op jit(solution)/shard_map/all_to_all | solution.py:28
  24.1 19.3 %all-to-all-done = bf16[32,32,1024]{2,1,0:T(8,128)(2,1)} async-done(((bf16[32,32,1024]{2,1,0:T(8,128)(2,1)}), bf16[32,32,1024]{2,1,0:T(8,128)(2,1)}, u32[]{:S(2)}, u32[]{:S(2)}) %all-to-all-start) | async-done | bytes 2097184 | tf_op jit(solution)/shard_map/all_to_all | solution.py:28
  48.0 5.6 %all-to-all-start.1 = ((bf16[16,192,512]{2,1,0:T(8,128)(2,1)}), bf16[16,192,512]{2,1,0:T(8,128)(2,1)}, u32[]{:S(2)}, u32[]{:S(2)}) async-start(bf16[16,192,512]{2,1,0:T(8,128)(2,1)} %pad_maximum_fusion), calls=%async_computation.1 | async-start | bytes 6291456 | tf_op jit(solution)/shard_map/all_to_all | solution.py:32
  53.6 3.2 %shard_map.95 = (bf16[128,1024]{1,0:T(8,128)(2,1)S(1)}, bf16[128,1024]{1,0:T(8,128)(2,1)S(1)}, bf16[128,1024]{1,0:T(8,128)(2,1)S(1)}, bf16[128,1024]{1,0:T(8,128...) custom-call(bf16[512,1024]{1,0:T(8,128)(2,1)S(1)} %bitcast.161, ...), custom_call_target="tpu_custom_call" | custom-call | tf_op jit(solution)/shard_map/pallas_call | solution.py:115
  56.9 3.4 %collective-permute-start.2 = (bf16[128,1024]{1,0:T(8,128)(2,1)S(1)}, bf16[128,1024]{1,0:T(8,128)(2,1)S(1)}, u32[]{:S(2)}, u32[]{:S(2)}) collective-permute-start(bf16[128,1024]{1,0:T(8,128)(2,1)S(1)} %get-tuple-element.47), channel_id=1, source_target_pairs={{0,64},{32,96},{64,128},{96,160},{128,192},{160,224},{192,0},{224,... | collective-permute-start | bytes 786440 | tf_op jit(solution)/shard_map/ppermute | solution.py:42
  62.4 2.8 %collective-permute-start.1 = (bf16[128,1024]{1,0:T(8,128)(2,1)S(1)}, bf16[128,1024]{1,0:T(8,128)(2,1)S(1)}, u32[]{:S(2)}, u32[]{:S(2)}) collective-permute-start(bf16[128,1024]{1,0:T(8,128)(2,1)S(1)} %get-tuple-element.45), channel_id=1, source_target_pairs={{0,192},{32,224},{64,0},{96,32},{128,64},{160,96},{192,128},{224,1... | collective-permute-start | bytes 786440 | tf_op jit(solution)/shard_map/ppermute | solution.py:42
  65.3 4.0 %collective-permute-done.2 = bf16[128,1024]{1,0:T(8,128)(2,1)S(1)} collective-permute-done((bf16[128,1024]{1,0:T(8,128)(2,1)S(1)}, bf16[128,1024]{1,0:T(8,128)(2,1)S(1)}, u32[]{:S(2)}, u32[]{:S(2)}) %collective-permute-start.2) | collective-permute-done | bytes 262176 | tf_op jit(solution)/shard_map/ppermute | solution.py:42
  69.2 6.4 %collective-permute-done.3 = bf16[128,1024]{1,0:T(8,128)(2,1)S(1)} collective-permute-done((bf16[128,1024]{1,0:T(8,128)(2,1)S(1)}, bf16[128,1024]{1,0:T(8,128)(2,1)S(1)}, u32[]{:S(2)}, u32[]{:S(2)}) %collective-permute-start.3) | collective-permute-done | bytes 262176 | tf_op jit(solution)/shard_map/ppermute | solution.py:42
  76.7 4.3 %collective-permute-start.4 = (bf16[128,1024]{1,0:T(8,128)(2,1)}, bf16[128,1024]{1,0:T(8,128)(2,1)}, u32[]{:S(2)}, u32[]{:S(2)}) collective-permute-start(bf16[128,1024]{1,0:T(8,128)(2,1)} %get-tuple-element.52), channel_id=1, source_target_pairs={{0,64},{32,96},{64,128},{96,160},{128,192},{160,224},{192,0},{224,... | collective-permute-start | bytes 786440 | tf_op jit(solution)/shard_map/ppermute | solution.py:42
  84.6 3.9 %collective-permute-start.6 = (bf16[128,1024]{1,0:T(8,128)(2,1)}, bf16[128,1024]{1,0:T(8,128)(2,1)}, u32[]{:S(2)}, u32[]{:S(2)}) collective-permute-start(bf16[128,1024]{1,0:T(8,128)(2,1)} %get-tuple-element.55), channel_id=1, source_target_pairs={{0,192},{32,224},{64,0},{96,32},{128,64},{160,96},{192,128},{224,1... | collective-permute-start | bytes 786440 | tf_op jit(solution)/shard_map/ppermute | solution.py:42
  90.6 6.2 %all-to-all-done.1 = bf16[16,192,512]{2,1,0:T(8,128)(2,1)} async-done(((bf16[16,192,512]{2,1,0:T(8,128)(2,1)}), bf16[16,192,512]{2,1,0:T(8,128)(2,1)}, u32[]{:S(2)}, u32[]{:S(2)}) %all-to-all-start.1) | async-done | bytes 3145760 | tf_op jit(solution)/shard_map/all_to_all | solution.py:32
  97.7 3.8 %collective-permute-start.7 = (bf16[128,512]{1,0:T(8,128)(2,1)S(1)}, bf16[128,512]{1,0:T(8,128)(2,1)S(1)}, u32[]{:S(2)}, u32[]{:S(2)}) collective-permute-start(bf16[128,512]{1,0:T(8,128)(2,1)S(1)} %dynamic-slice_bitcast_fusion), channel_id=1, source_target_pairs={{0,16},{1,17},{2,18},{3,19},{4,20},{5,21},{6,22},{7,23},{8,24},{9,... | collective-permute-start | bytes 393224 | tf_op jit(solution)/shard_map/ppermute | solution.py:38
  108.3 4.8 %collective-permute-start.11 = (bf16[2,32,512]{2,1,0:T(8,128)(2,1)S(1)}, bf16[2,32,512]{2,1,0:T(8,128)(2,1)S(1)}, u32[]{:S(2)}, u32[]{:S(2)}) collective-permute-start(bf16[2,32,512]{2,1,0:T(8,128)(2,1)S(1)} %fusion.20), channel_id=1, source_target_pairs={{0,192},{32,224},{64,0},{96,32},{128,64},{160,96},{192,128},{224,1... | collective-permute-start | bytes 196616 | tf_op jit(solution)/shard_map/ppermute | solution.py:42
  117.2 6.1 %collective-permute-done.10 = bf16[2,32,512]{2,1,0:T(8,128)(2,1)S(1)} collective-permute-done((bf16[2,32,512]{2,1,0:T(8,128)(2,1)S(1)}, bf16[2,32,512]{2,1,0:T(8,128)(2,1)S(1)}, u32[]{:S(2)}, u32[]{:S(2)}) %collective-permute-start.10) | collective-permute-done | bytes 65568 | tf_op jit(solution)/shard_map/ppermute | solution.py:42
  128.9 3.0 %collective-permute-done.13 = bf16[128,512]{1,0:T(8,128)(2,1)S(1)} collective-permute-done((bf16[128,512]{1,0:T(8,128)(2,1)S(1)}, bf16[128,512]{1,0:T(8,128)(2,1)S(1)}, u32[]{:S(2)}, u32[]{:S(2)}) %collective-permute-start.13) | collective-permute-done | bytes 131104 | tf_op jit(solution)/shard_map/ppermute | solution.py:38
  137.8 10.4 %all-to-all-start.2 = ((bf16[16,192,512]{2,1,0:T(8,128)(2,1)}), bf16[16,192,512]{2,1,0:T(8,128)(2,1)}, u32[]{:S(2)}, u32[]{:S(2)}) async-start(bf16[16,192,512]{2,1,0:T(8,128)(2,1)} %pad_maximum_fusion.1), calls=%async_computation.2 | async-start | bytes 6291456 | tf_op jit(solution)/shard_map/all_to_all | solution.py:32
  148.2 5.6 %collective-permute-done.15 = bf16[2,128,1024]{2,1,0:T(8,128)(2,1)S(1)} collective-permute-done((bf16[2,128,1024]{2,1,0:T(8,128)(2,1)}, bf16[2,128,1024]{2,1,0:T(8,128)(2,1)S(1)}, u32[]{:S(2)}, u32[]{:S(2)}) %collective-permute-start.15) | collective-permute-done | bytes 524320 | tf_op jit(solution)/shard_map/ppermute | solution.py:42
  154.1 2.8 %collective-permute-start.16 = (bf16[128,1024]{1,0:T(8,128)(2,1)S(1)}, bf16[128,1024]{1,0:T(8,128)(2,1)S(1)}, u32[]{:S(2)}, u32[]{:S(2)}) collective-permute-start(bf16[128,1024]{1,0:T(8,128)(2,1)S(1)} %slice_bitcast_fusion.1), channel_id=1, source_target_pairs={{0,64},{32,96},{64,128},{96,160},{128,192},{160,224},{192,0},{224,... | collective-permute-start | bytes 786440 | tf_op jit(solution)/shard_map/ppermute | solution.py:42
  165.0 3.3 %collective-permute-done.16 = bf16[128,1024]{1,0:T(8,128)(2,1)S(1)} collective-permute-done((bf16[128,1024]{1,0:T(8,128)(2,1)S(1)}, bf16[128,1024]{1,0:T(8,128)(2,1)S(1)}, u32[]{:S(2)}, u32[]{:S(2)}) %collective-permute-start.16) | collective-permute-done | bytes 262176 | tf_op jit(solution)/shard_map/ppermute | solution.py:42
  173.6 16.0 %all-to-all-done.2 = bf16[16,192,512]{2,1,0:T(8,128)(2,1)} async-done(((bf16[16,192,512]{2,1,0:T(8,128)(2,1)}), bf16[16,192,512]{2,1,0:T(8,128)(2,1)}, u32[]{:S(2)}, u32[]{:S(2)}) %all-to-all-start.2) | async-done | bytes 3145760 | tf_op jit(solution)/shard_map/all_to_all | solution.py:32
  189.7 9.8 %all-to-all-start.3 = ((bf16[32,32,1024]{2,1,0:T(8,128)(2,1)}), bf16[32,32,1024]{2,1,0:T(8,128)(2,1)}, u32[]{:S(2)}, u32[]{:S(2)}) async-start(bf16[32,32,1024]{2,1,0:T(8,128)(2,1)} %bitcast.51), calls=%async_computation.3 | async-start | bytes 4194304 | tf_op jit(solution)/shard_map/all_to_all | solution.py:28
  200.1 2.7 %slice_select_fusion = (bf16[16,64,512]{2,1,0:T(8,128)(2,1)}, bf16[16,64,512]{2,1,0:T(8,128)(2,1)S(1)}) fusion(bf16[16,192,512]{2,1,0:T(8,128)(2,1)} %all-to-all-done.2, pred[]{:T(512)S(6)} %eq.80), kind=kLoop, calls=%fused_computation.40 | loop fusion | flops 1048576 | bytes 4194305 | tf_op jit(solution)/shard_map/jit(_where)/select_n | solution.py:311
  204.4 3.0 %copy.39 = f32[1024,512]{0,1:T(8,128)} copy(f32[1024,512]{1,0:T(8,128)} %bitcast_convert_fusion) | data formatting | bytes 4194304 | tf_op jit(solution)/shard_map/convert_element_type | solution.py:316
  216.9 9.3 %all-to-all-done.3 = bf16[32,32,1024]{2,1,0:T(8,128)(2,1)} async-done(((bf16[32,32,1024]{2,1,0:T(8,128)(2,1)}), bf16[32,32,1024]{2,1,0:T(8,128)(2,1)}, u32[]{:S(2)}, u32[]{:S(2)}) %all-to-all-start.3) | async-done | bytes 2097184 | tf_op jit(solution)/shard_map/all_to_all | solution.py:28
  (166 shorter events, 77.1 us)
Async XLA Ops:
  6.7 36.7 %all-to-all-start = ((bf16[32,32,1024]{2,1,0:T(8,128)(2,1)}), bf16[32,32,1024]{2,1,0:T(8,128)(2,1)}, u32[]{:S(2)}, u32[]{:S(2)}) async-start(bf16[32,32,1024]{2,1,0:T(8,128)(2,1)} %bitcast.157), calls=%async_computation | async-start | bytes 4194304 | tf_op jit(solution)/shard_map/all_to_all | solution.py:28
  48.0 5.7 %collective-permute-start = (bf16[8,128,1024]{2,1,0:T(8,128)(2,1)}, bf16[8,128,1024]{2,1,0:T(8,128)(2,1)}, u32[]{:S(2)}, u32[]{:S(2)}) collective-permute-start(bf16[8,128,1024]{2,1,0:T(8,128)(2,1)} %shard_map.94), channel_id=1, source_target_pairs={{0,32},{32,0},{64,96},{96,64},{128,160},{160,128},{192,224},{224,1... | collective-permute-start | bytes 6291464 | tf_op jit(solution)/shard_map/ppermute | solution.py:42
  48.0 48.8 %all-to-all-start.1 = ((bf16[16,192,512]{2,1,0:T(8,128)(2,1)}), bf16[16,192,512]{2,1,0:T(8,128)(2,1)}, u32[]{:S(2)}, u32[]{:S(2)}) async-start(bf16[16,192,512]{2,1,0:T(8,128)(2,1)} %pad_maximum_fusion), calls=%async_computation.1 | async-start | bytes 6291456 | tf_op jit(solution)/shard_map/all_to_all | solution.py:32
  56.9 12.4 %collective-permute-start.2 = (bf16[128,1024]{1,0:T(8,128)(2,1)S(1)}, bf16[128,1024]{1,0:T(8,128)(2,1)S(1)}, u32[]{:S(2)}, u32[]{:S(2)}) collective-permute-start(bf16[128,1024]{1,0:T(8,128)(2,1)S(1)} %get-tuple-element.47), channel_id=1, source_target_pairs={{0,64},{32,96},{64,128},{96,160},{128,192},{160,224},{192,0},{224,... | collective-permute-start | bytes 786440 | tf_op jit(solution)/shard_map/ppermute | solution.py:42
  60.2 15.4 %collective-permute-start.3 = (bf16[128,1024]{1,0:T(8,128)(2,1)S(1)}, bf16[128,1024]{1,0:T(8,128)(2,1)S(1)}, u32[]{:S(2)}, u32[]{:S(2)}) collective-permute-start(bf16[128,1024]{1,0:T(8,128)(2,1)S(1)} %get-tuple-element.48), channel_id=1, source_target_pairs={{0,192},{32,224},{64,0},{96,32},{128,64},{160,96},{192,128},{224,1... | collective-permute-start | bytes 786440 | tf_op jit(solution)/shard_map/ppermute | solution.py:42
  62.4 26.1 %collective-permute-start.1 = (bf16[128,1024]{1,0:T(8,128)(2,1)S(1)}, bf16[128,1024]{1,0:T(8,128)(2,1)S(1)}, u32[]{:S(2)}, u32[]{:S(2)}) collective-permute-start(bf16[128,1024]{1,0:T(8,128)(2,1)S(1)} %get-tuple-element.45), channel_id=1, source_target_pairs={{0,192},{32,224},{64,0},{96,32},{128,64},{160,96},{192,128},{224,1... | collective-permute-start | bytes 786440 | tf_op jit(solution)/shard_map/ppermute | solution.py:42
  76.7 11.9 %collective-permute-start.4 = (bf16[128,1024]{1,0:T(8,128)(2,1)}, bf16[128,1024]{1,0:T(8,128)(2,1)}, u32[]{:S(2)}, u32[]{:S(2)}) collective-permute-start(bf16[128,1024]{1,0:T(8,128)(2,1)} %get-tuple-element.52), channel_id=1, source_target_pairs={{0,64},{32,96},{64,128},{96,160},{128,192},{160,224},{192,0},{224,... | collective-permute-start | bytes 786440 | tf_op jit(solution)/shard_map/ppermute | solution.py:42
  84.3 22.5 %collective-permute-start.5 = (bf16[128,1024]{1,0:T(8,128)(2,1)S(1)}, bf16[128,1024]{1,0:T(8,128)(2,1)}, u32[]{:S(2)}, u32[]{:S(2)}) collective-permute-start(bf16[128,1024]{1,0:T(8,128)(2,1)S(1)} %get-tuple-element.54), channel_id=1, source_target_pairs={{0,64},{32,96},{64,128},{96,160},{128,192},{160,224},{192,0},{224,... | collective-permute-start | bytes 786440 | tf_op jit(solution)/shard_map/ppermute | solution.py:42
  84.6 22.2 %collective-permute-start.6 = (bf16[128,1024]{1,0:T(8,128)(2,1)}, bf16[128,1024]{1,0:T(8,128)(2,1)}, u32[]{:S(2)}, u32[]{:S(2)}) collective-permute-start(bf16[128,1024]{1,0:T(8,128)(2,1)} %get-tuple-element.55), channel_id=1, source_target_pairs={{0,192},{32,224},{64,0},{96,32},{128,64},{160,96},{192,128},{224,1... | collective-permute-start | bytes 786440 | tf_op jit(solution)/shard_map/ppermute | solution.py:42
  97.7 7.3 %collective-permute-start.7 = (bf16[128,512]{1,0:T(8,128)(2,1)S(1)}, bf16[128,512]{1,0:T(8,128)(2,1)S(1)}, u32[]{:S(2)}, u32[]{:S(2)}) collective-permute-start(bf16[128,512]{1,0:T(8,128)(2,1)S(1)} %dynamic-slice_bitcast_fusion), channel_id=1, source_target_pairs={{0,16},{1,17},{2,18},{3,19},{4,20},{5,21},{6,22},{7,23},{8,24},{9,... | collective-permute-start | bytes 393224 | tf_op jit(solution)/shard_map/ppermute | solution.py:38
  106.6 1.7 collective-permute-start.8
  108.3 8.9 %collective-permute-start.11 = (bf16[2,32,512]{2,1,0:T(8,128)(2,1)S(1)}, bf16[2,32,512]{2,1,0:T(8,128)(2,1)S(1)}, u32[]{:S(2)}, u32[]{:S(2)}) collective-permute-start(bf16[2,32,512]{2,1,0:T(8,128)(2,1)S(1)} %fusion.20), channel_id=1, source_target_pairs={{0,192},{32,224},{64,0},{96,32},{128,64},{160,96},{192,128},{224,1... | collective-permute-start | bytes 196616 | tf_op jit(solution)/shard_map/ppermute | solution.py:42
  113.1 10.2 %collective-permute-start.10 = (bf16[2,32,512]{2,1,0:T(8,128)(2,1)S(1)}, bf16[2,32,512]{2,1,0:T(8,128)(2,1)S(1)}, u32[]{:S(2)}, u32[]{:S(2)}) collective-permute-start(bf16[2,32,512]{2,1,0:T(8,128)(2,1)S(1)} %fusion.20), channel_id=1, source_target_pairs={{0,128},{32,160},{64,192},{96,224},{128,0},{160,32},{192,64},{224,... | collective-permute-start | bytes 196616 | tf_op jit(solution)/shard_map/ppermute | solution.py:42
  114.8 8.5 %collective-permute-start.9 = (bf16[2,32,512]{2,1,0:T(8,128)(2,1)S(1)}, bf16[2,32,512]{2,1,0:T(8,128)(2,1)S(1)}, u32[]{:S(2)}, u32[]{:S(2)}) collective-permute-start(bf16[2,32,512]{2,1,0:T(8,128)(2,1)S(1)} %fusion.20), channel_id=1, source_target_pairs={{0,64},{32,96},{64,128},{96,160},{128,192},{160,224},{192,0},{224,... | collective-permute-start | bytes 196616 | tf_op jit(solution)/shard_map/ppermute | solution.py:42
  126.2 5.7 %collective-permute-start.13 = (bf16[128,512]{1,0:T(8,128)(2,1)S(1)}, bf16[128,512]{1,0:T(8,128)(2,1)S(1)}, u32[]{:S(2)}, u32[]{:S(2)}) collective-permute-start(bf16[128,512]{1,0:T(8,128)(2,1)S(1)} %pad_maximum_fusion.12), channel_id=1, source_target_pairs={{0,16},{1,17},{2,18},{3,19},{4,20},{5,21},{6,22},{7,23},{8,24},{9,... | collective-permute-start | bytes 393224 | tf_op jit(solution)/shard_map/ppermute | solution.py:38
  132.0 5.8 %collective-permute-start.18 = (bf16[2,128,1024]{2,1,0:T(8,128)(2,1)}, bf16[2,128,1024]{2,1,0:T(8,128)(2,1)}, u32[]{:S(2)}, u32[]{:S(2)}) collective-permute-start(bf16[2,128,1024]{2,1,0:T(8,128)(2,1)} %pad_maximum_fusion.11), channel_id=1, source_target_pairs={{0,32},{32,0},{64,96},{96,64},{128,160},{160,128},{192,224},{224,1... | collective-permute-start | bytes 1572872 | tf_op jit(solution)/shard_map/ppermute | solution.py:42
  132.4 21.4 %collective-permute-start.15 = (bf16[2,128,1024]{2,1,0:T(8,128)(2,1)}, bf16[2,128,1024]{2,1,0:T(8,128)(2,1)S(1)}, u32[]{:S(2)}, u32[]{:S(2)}) collective-permute-start(bf16[2,128,1024]{2,1,0:T(8,128)(2,1)} %pad_maximum_fusion.11), channel_id=1, source_target_pairs={{0,192},{32,224},{64,0},{96,32},{128,64},{160,96},{192,128},{224,1... | collective-permute-start | bytes 1572872 | tf_op jit(solution)/shard_map/ppermute | solution.py:42
  134.9 18.9 %collective-permute-start.14 = (bf16[2,128,1024]{2,1,0:T(8,128)(2,1)}, bf16[2,128,1024]{2,1,0:T(8,128)(2,1)S(1)}, u32[]{:S(2)}, u32[]{:S(2)}) collective-permute-start(bf16[2,128,1024]{2,1,0:T(8,128)(2,1)} %pad_maximum_fusion.11), channel_id=1, source_target_pairs={{0,64},{32,96},{64,128},{96,160},{128,192},{160,224},{192,0},{224,... | collective-permute-start | bytes 1572872 | tf_op jit(solution)/shard_map/ppermute | solution.py:42
  137.8 51.9 %all-to-all-start.2 = ((bf16[16,192,512]{2,1,0:T(8,128)(2,1)}), bf16[16,192,512]{2,1,0:T(8,128)(2,1)}, u32[]{:S(2)}, u32[]{:S(2)}) async-start(bf16[16,192,512]{2,1,0:T(8,128)(2,1)} %pad_maximum_fusion.1), calls=%async_computation.2 | async-start | bytes 6291456 | tf_op jit(solution)/shard_map/all_to_all | solution.py:32
  154.0 7.5 %collective-permute-start.19 = (bf16[2,2,128,1024]{3,2,1,0:T(8,128)(2,1)S(1)}, bf16[2,2,128,1024]{3,2,1,0:T(8,128)(2,1)S(1)}, u32[]{:S(2)}, u32[]{:S(2)}) collective-permute-start(bf16[2,2,128,1024]{3,2,1,0:T(8,128)(2,1)S(1)} %pad_maximum_fusion.7), channel_id=1, source_target_pairs={{0,32},{32,0},{64,96},{96,64},{128,160},{160,128},{192,224},{224,1... | collective-permute-start | bytes 3145736 | tf_op jit(solution)/shard_map/ppermute | solution.py:42
  154.1 14.2 %collective-permute-start.16 = (bf16[128,1024]{1,0:T(8,128)(2,1)S(1)}, bf16[128,1024]{1,0:T(8,128)(2,1)S(1)}, u32[]{:S(2)}, u32[]{:S(2)}) collective-permute-start(bf16[128,1024]{1,0:T(8,128)(2,1)S(1)} %slice_bitcast_fusion.1), channel_id=1, source_target_pairs={{0,64},{32,96},{64,128},{96,160},{128,192},{160,224},{192,0},{224,... | collective-permute-start | bytes 786440 | tf_op jit(solution)/shard_map/ppermute | solution.py:42
  156.8 11.5 %collective-permute-start.17 = (bf16[128,1024]{1,0:T(8,128)(2,1)S(1)}, bf16[128,1024]{1,0:T(8,128)(2,1)S(1)}, u32[]{:S(2)}, u32[]{:S(2)}) collective-permute-start(bf16[128,1024]{1,0:T(8,128)(2,1)S(1)} %slice_bitcast_fusion), channel_id=1, source_target_pairs={{0,192},{32,224},{64,0},{96,32},{128,64},{160,96},{192,128},{224,1... | collective-permute-start | bytes 786440 | tf_op jit(solution)/shard_map/ppermute | solution.py:42
  168.4 2.2 collective-permute-start.20
  189.7 36.6 %all-to-all-start.3 = ((bf16[32,32,1024]{2,1,0:T(8,128)(2,1)}), bf16[32,32,1024]{2,1,0:T(8,128)(2,1)}, u32[]{:S(2)}, u32[]{:S(2)}) async-start(bf16[32,32,1024]{2,1,0:T(8,128)(2,1)} %bitcast.51), calls=%async_computation.3 | async-start | bytes 4194304 | tf_op jit(solution)/shard_map/all_to_all | solution.py:28
  (30 other events, 137.7 us)

commit v2 on v1

--- a/solution.py
+++ b/solution.py
@@ -198,6 +198,20 @@
     return jnp.concatenate([first, second], 1)
 
 
+def combine(collect, table, mixed_late, tokens_late):
+    def body(collect_ref, table_ref, mixed_late_ref, tokens_late_ref, mixed_ref, tokens_ref):
+        mixed = mm(collect_ref[:256], table_ref[:, :512], 1, 0)
+        mixed_ref[...] = (mixed[:128] + mixed[128:] + mixed_late_ref[...]).astype(BF16)
+        back = mm(collect_ref[256:], table_ref[:, 512:], 1, 0)
+        tokens_ref[...] = (back + tokens_late_ref[...]).astype(BF16)
+
+    return pl.pallas_call(
+        body,
+        out_shape=[jax.ShapeDtypeStruct((128, 512), BF16)] * 2,
+        compiler_params=params(),
+    )(collect, table, mixed_late, tokens_late)
+
+
 def two_parts(block):
     high = block.astype(BF16)
     return high, (block - high.astype(F32)).astype(BF16)
@@ -285,8 +299,8 @@
     weight_grads = jnp.concatenate(
         [mm(hidden_hot, s_hot, 1, 0), mm(grad_hot, x_hot, 1, 0)], 0
     ).astype(BF16)
+    share, weight_grads = after(share, weight_grads)
     weight_grads = add16(weight_grads, partner(weight_grads))
-    share, weight_grads = after(share, weight_grads)
     hot_back = jnp.concatenate([split(out_hot), split(in_hot), spread(weight_grads)], 1)
     pieces, used, hot_back = all_blocks(
         share, hot_back, lambda pairs: finish(pairs, down_home, up_home)
@@ -319,12 +333,10 @@
     mixed_late = mm(high_late, out_late, 0, 0) + mm(low_late, out_late, 0, 0)
     tokens_late = mm(choose_late, in_late, 0, 0)
 
-    total = mm(collect, table, 1, 0)
-    mixed = total[:rows, :width] + total[rows : 2 * rows, :width] + mixed_late
-    d_tokens = total[2 * rows :, width:] + tokens_late
+    mixed, d_tokens = combine(collect, table, mixed_late, tokens_late)
     return (
-        mixed.astype(BF16),
-        d_tokens.astype(BF16),
+        mixed,
+        d_tokens,
         grad_up.astype(BF16)[None],
         grad_down.astype(BF16)[None],
     )

time: 232 us -> 230 us (level)
  waiting for transfers between devices: 83.8 us -> 66.2 us
  starting transfers between devices: 74.6 us -> 85.8 us
  matrix products: 12.1 us -> 7.12 us
  local copies, waits for them, and re-layouts: 15 us -> 19.4 us
  Pallas kernels: 12.3 us -> 16.6 us
    all_to_all x2, starting transfers between devices: 15.9 us -> 27 us  [exchange_in_plane(): lax.all_to_all(payload, 'expert', split_axis=0, concat_axis=0, tiled=True...]
    ppermute x19, waiting for transfers between devices: 27.7 us -> 20.6 us  [send(): return lax.ppermute(block, 'dp', pairs)]
    all_to_all x2, waiting for transfers between devices: 28.6 us -> 23.3 us  [exchange(): lax.all_to_all(payload, 'expert', split_axis=0, concat_axis=0, tiled=True)]
    dot_general x15 -> x14, matrix products: 12.1 us -> 7.12 us  [mm(): return lax.dot_general(left, right, dims, preferred_element_type=F32)]
    all_to_all x2, waiting for transfers between devices: 22.3 us -> 19.3 us  [exchange_in_plane(): lax.all_to_all(payload, 'expert', split_axis=0, concat_axis=0, tiled=True...]
    pallas_call x0 -> x1, Pallas kernels: none -> 2.82 us  [combine(): pl.pallas_call(body, out_shape=[jax.ShapeDtypeStruct((128, 512), BF16)] *...]
    unnamed x57 -> x65, local copies, waits for them, and re-layouts: 6.21 us -> 6.05 us
  transfers between devices with their start and end apart: 25 -> 25, of which waited for: 13 -> 12; matrix products, arithmetic and copies ran while one was open for 17% -> 19% of each run, Pallas kernels for 4% -> 4%
where the time goes in v2:
time: 230 us; the launch traced here: 229 us
  starting transfers between devices  85.8 us (37%)
  waiting for transfers between devices  66.2 us (29%)
  other arithmetic  29.2 us (13%)
  local copies, waits for them, and re-layouts  19.4 us (8%)
  Pallas kernels  16.6 us (7%)
  matrix products  7.12 us (3%)
  between operations  4.7 us (2%)
    ppermute x19, starting transfers between devices, send(): return lax.ppermute(block, 'dp', pairs)  33 us
    all_to_all x2, starting transfers between devices, exchange_in_plane(): lax.all_to_all(payload, 'expert', split_axis=0, concat_axis=0, tiled=True...  27 us
    all_to_all x2, waiting for transfers between devices, exchange(): lax.all_to_all(payload, 'expert', split_axis=0, concat_axis=0, tiled=True)  23.3 us
    ppermute x19, waiting for transfers between devices, send(): return lax.ppermute(block, 'dp', pairs)  20.6 us
    all_to_all x2, waiting for transfers between devices, exchange_in_plane(): lax.all_to_all(payload, 'expert', split_axis=0, concat_axis=0, tiled=True...  19.3 us
    all_to_all x2, starting transfers between devices, exchange(): lax.all_to_all(payload, 'expert', split_axis=0, concat_axis=0, tiled=True)  18.6 us
    ppermute x2, starting transfers between devices, partner(): return lax.ppermute(block, 'expert', PARTNER)  7.2 us
    dot_general x14, matrix products, mm(): return lax.dot_general(left, right, dims, preferred_element_type=F32)  7.12 us
  transfers between devices with their start and end apart: 25, of which 12 were waited for; matrix products, arithmetic and copies ran while one was open for 19% of the time, Pallas kernels for 4%

profile of v2, /device:TPU:2, one launch (start us, length us, event | category | flops | bytes accessed | tf_op | source)
XLA Modules:
  0.0 229.1 jit_solution(2874517267273253488)
XLA Ops:
  6.6 9.0 %all-to-all-start = ((bf16[32,32,1024]{2,1,0:T(8,128)(2,1)}), bf16[32,32,1024]{2,1,0:T(8,128)(2,1)}, u32[]{:S(2)}, u32[]{:S(2)}) async-start(bf16[32,32,1024]{2,1,0:T(8,128)(2,1)} %bitcast.8), calls=%async_computation | async-start | bytes 4194304 | tf_op jit(solution)/shard_map/all_to_all | solution.py:28
  23.0 20.2 %all-to-all-done = bf16[32,32,1024]{2,1,0:T(8,128)(2,1)} async-done(((bf16[32,32,1024]{2,1,0:T(8,128)(2,1)}), bf16[32,32,1024]{2,1,0:T(8,128)(2,1)}, u32[]{:S(2)}, u32[]{:S(2)}) %all-to-all-start) | async-done | bytes 2097184 | tf_op jit(solution)/shard_map/all_to_all | solution.py:28
  43.1 2.8 %constant_dynamic-slice_fusion = (bf16[1,16,4,8,1024]{4,3,2,1,0:T(8,128)(2,1)S(1)}, bf16[1,16,4,8,1024]{4,3,2,1,0:T(8,128)(2,1)}) fusion(bf16[2,16,4,8,1024]{4,3,2,1,0:T(8,128)(2,1)} %bitcast.11, s32[]{:T(128)S(6)} %select_n.140, s32[]{:T(128)S(6)} %select_n.139), kind=kLoop, calls=%fused_computation.107 | loop fusion | bytes 4194312 | tf_op jit(solution)/shard_map/jit(dynamic_index_in_dim)/dynamic_slice | solution.py:54
  46.0 2.7 %shard_map.94 = bf16[8,128,1024]{2,1,0:T(8,128)(2,1)} custom-call(bf16[512,1024]{1,0:T(8,128)(2,1)S(1)} %bitcast.135, bf16[512,1024]{1,0:T(8,128)(2,1)S(1)} %bitcast.122, bf16[1024,512]{1,0:T(8,128)(2,1)S(1)} %bitcast.129), custom_call_target="tpu_custom_call" | custom-call | tf_op jit(solution)/shard_map/pallas_call | solution.py:98
  48.7 5.5 %all-to-all-start.1 = ((bf16[16,192,512]{2,1,0:T(8,128)(2,1)}), bf16[16,192,512]{2,1,0:T(8,128)(2,1)}, u32[]{:S(2)}, u32[]{:S(2)}) async-start(bf16[16,192,512]{2,1,0:T(8,128)(2,1)} %pad_maximum_fusion), calls=%async_computation.1 | async-start | bytes 6291456 | tf_op jit(solution)/shard_map/all_to_all | solution.py:32
  55.6 3.4 %shard_map.95 = (bf16[128,1024]{1,0:T(8,128)(2,1)S(1)}, bf16[128,1024]{1,0:T(8,128)(2,1)S(1)}, bf16[128,1024]{1,0:T(8,128)(2,1)S(1)}, bf16[128,1024]{1,0:T(8,128...) custom-call(bf16[512,1024]{1,0:T(8,128)(2,1)S(1)} %bitcast.138, ...), custom_call_target="tpu_custom_call" | custom-call | tf_op jit(solution)/shard_map/pallas_call | solution.py:115
  59.0 3.3 %collective-permute-start.2 = (bf16[128,1024]{1,0:T(8,128)(2,1)S(1)}, bf16[128,1024]{1,0:T(8,128)(2,1)S(1)}, u32[]{:S(2)}, u32[]{:S(2)}) collective-permute-start(bf16[128,1024]{1,0:T(8,128)(2,1)S(1)} %get-tuple-element.49), channel_id=1, source_target_pairs={{0,64},{32,96},{64,128},{96,160},{128,192},{160,224},{192,0},{224,... | collective-permute-start | bytes 786440 | tf_op jit(solution)/shard_map/ppermute | solution.py:42
  64.5 2.8 %collective-permute-start.1 = (bf16[128,1024]{1,0:T(8,128)(2,1)}, bf16[128,1024]{1,0:T(8,128)(2,1)}, u32[]{:S(2)}, u32[]{:S(2)}) collective-permute-start(bf16[128,1024]{1,0:T(8,128)(2,1)} %get-tuple-element.47), channel_id=1, source_target_pairs={{0,192},{32,224},{64,0},{96,32},{128,64},{160,96},{192,128},{224,1... | collective-permute-start | bytes 786440 | tf_op jit(solution)/shard_map/ppermute | solution.py:42
  67.3 4.0 %collective-permute-done.2 = bf16[128,1024]{1,0:T(8,128)(2,1)S(1)} collective-permute-done((bf16[128,1024]{1,0:T(8,128)(2,1)S(1)}, bf16[128,1024]{1,0:T(8,128)(2,1)S(1)}, u32[]{:S(2)}, u32[]{:S(2)}) %collective-permute-start.2) | collective-permute-done | bytes 262176 | tf_op jit(solution)/shard_map/ppermute | solution.py:42
  71.3 6.3 %collective-permute-done.3 = bf16[128,1024]{1,0:T(8,128)(2,1)S(1)} collective-permute-done((bf16[128,1024]{1,0:T(8,128)(2,1)S(1)}, bf16[128,1024]{1,0:T(8,128)(2,1)S(1)}, u32[]{:S(2)}, u32[]{:S(2)}) %collective-permute-start.3) | collective-permute-done | bytes 262176 | tf_op jit(solution)/shard_map/ppermute | solution.py:42
  78.6 4.2 %collective-permute-start.4 = (bf16[128,1024]{1,0:T(8,128)(2,1)}, bf16[128,1024]{1,0:T(8,128)(2,1)}, u32[]{:S(2)}, u32[]{:S(2)}) collective-permute-start(bf16[128,1024]{1,0:T(8,128)(2,1)} %get-tuple-element.54), channel_id=1, source_target_pairs={{0,64},{32,96},{64,128},{96,160},{128,192},{160,224},{192,0},{224,... | collective-permute-start | bytes 786440 | tf_op jit(solution)/shard_map/ppermute | solution.py:42
  86.6 3.8 %collective-permute-start.6 = (bf16[128,1024]{1,0:T(8,128)(2,1)}, bf16[128,1024]{1,0:T(8,128)(2,1)}, u32[]{:S(2)}, u32[]{:S(2)}) collective-permute-start(bf16[128,1024]{1,0:T(8,128)(2,1)} %get-tuple-element.57), channel_id=1, source_target_pairs={{0,192},{32,224},{64,0},{96,32},{128,64},{160,96},{192,128},{224,1... | collective-permute-start | bytes 786440 | tf_op jit(solution)/shard_map/ppermute | solution.py:42
  92.5 5.0 %all-to-all-done.1 = bf16[16,192,512]{2,1,0:T(8,128)(2,1)} async-done(((bf16[16,192,512]{2,1,0:T(8,128)(2,1)}), bf16[16,192,512]{2,1,0:T(8,128)(2,1)}, u32[]{:S(2)}, u32[]{:S(2)}) %all-to-all-start.1) | async-done | bytes 3145760 | tf_op jit(solution)/shard_map/all_to_all | solution.py:32
  98.4 5.0 %collective-permute-start.7 = (bf16[128,512]{1,0:T(8,128)(2,1)S(1)}, bf16[128,512]{1,0:T(8,128)(2,1)S(1)}, u32[]{:S(2)}, u32[]{:S(2)}) collective-permute-start(bf16[128,512]{1,0:T(8,128)(2,1)S(1)} %dynamic-slice_bitcast_fusion), channel_id=1, source_target_pairs={{0,16},{1,17},{2,18},{3,19},{4,20},{5,21},{6,22},{7,23},{8,24},{9,... | collective-permute-start | bytes 393224 | tf_op jit(solution)/shard_map/ppermute | solution.py:38
  111.5 3.4 %collective-permute-start.11 = (bf16[2,32,512]{2,1,0:T(8,128)(2,1)}, bf16[2,32,512]{2,1,0:T(8,128)(2,1)}, u32[]{:S(2)}, u32[]{:S(2)}) collective-permute-start(bf16[2,32,512]{2,1,0:T(8,128)(2,1)} %fusion.13), channel_id=1, source_target_pairs={{0,192},{32,224},{64,0},{96,32},{128,64},{160,96},{192,128},{224,1... | collective-permute-start | bytes 196616 | tf_op jit(solution)/shard_map/ppermute | solution.py:42
  114.9 2.7 %collective-permute-start.10 = (bf16[2,32,512]{2,1,0:T(8,128)(2,1)}, bf16[2,32,512]{2,1,0:T(8,128)(2,1)}, u32[]{:S(2)}, u32[]{:S(2)}) collective-permute-start(bf16[2,32,512]{2,1,0:T(8,128)(2,1)} %fusion.13), channel_id=1, source_target_pairs={{0,128},{32,160},{64,192},{96,224},{128,0},{160,32},{192,64},{224,... | collective-permute-start | bytes 196616 | tf_op jit(solution)/shard_map/ppermute | solution.py:42
  119.4 6.1 %collective-permute-done.10 = bf16[2,32,512]{2,1,0:T(8,128)(2,1)} collective-permute-done((bf16[2,32,512]{2,1,0:T(8,128)(2,1)}, bf16[2,32,512]{2,1,0:T(8,128)(2,1)}, u32[]{:S(2)}, u32[]{:S(2)}) %collective-permute-start.10) | collective-permute-done | bytes 65568 | tf_op jit(solution)/shard_map/ppermute | solution.py:42
  138.0 21.4 %all-to-all-start.2 = ((bf16[16,192,512]{2,1,0:T(8,128)(2,1)}), bf16[16,192,512]{2,1,0:T(8,128)(2,1)}, u32[]{:S(2)}, u32[]{:S(2)}) async-start(bf16[16,192,512]{2,1,0:T(8,128)(2,1)} %pad_maximum_fusion.1), calls=%async_computation.2 | async-start | bytes 6291456 | tf_op jit(solution)/shard_map/all_to_all | solution.py:32
  163.8 3.7 %collective-permute-start.16 = (bf16[128,1024]{1,0:T(8,128)(2,1)S(1)}, bf16[128,1024]{1,0:T(8,128)(2,1)S(1)}, u32[]{:S(2)}, u32[]{:S(2)}) collective-permute-start(bf16[128,1024]{1,0:T(8,128)(2,1)S(1)} %slice_bitcast_fusion), channel_id=1, source_target_pairs={{0,192},{32,224},{64,0},{96,32},{128,64},{160,96},{192,128},{224,1... | collective-permute-start | bytes 786440 | tf_op jit(solution)/shard_map/ppermute | solution.py:42
  179.6 14.3 %all-to-all-done.2 = bf16[16,192,512]{2,1,0:T(8,128)(2,1)} async-done(((bf16[16,192,512]{2,1,0:T(8,128)(2,1)}), bf16[16,192,512]{2,1,0:T(8,128)(2,1)}, u32[]{:S(2)}, u32[]{:S(2)}) %all-to-all-start.2) | async-done | bytes 3145760 | tf_op jit(solution)/shard_map/all_to_all | solution.py:32
  195.5 9.6 %all-to-all-start.3 = ((bf16[32,32,1024]{2,1,0:T(8,128)(2,1)}), bf16[32,32,1024]{2,1,0:T(8,128)(2,1)}, u32[]{:S(2)}, u32[]{:S(2)}) async-start(bf16[32,32,1024]{2,1,0:T(8,128)(2,1)} %bitcast.51), calls=%async_computation.3 | async-start | bytes 4194304 | tf_op jit(solution)/shard_map/all_to_all | solution.py:28
  210.1 3.1 %copy.42 = f32[1024,512]{0,1:T(8,128)} copy(f32[1024,512]{1,0:T(8,128)} %bitcast_convert_fusion) | data formatting | bytes 4194304 | tf_op jit(solution)/shard_map/convert_element_type | solution.py:330
  223.1 3.1 %all-to-all-done.3 = bf16[32,32,1024]{2,1,0:T(8,128)(2,1)} async-done(((bf16[32,32,1024]{2,1,0:T(8,128)(2,1)}), bf16[32,32,1024]{2,1,0:T(8,128)(2,1)}, u32[]{:S(2)}, u32[]{:S(2)}) %all-to-all-start.3) | async-done | bytes 2097184 | tf_op jit(solution)/shard_map/all_to_all | solution.py:28
  226.2 2.8 %shard_map.100 = (bf16[128,512]{1,0:T(8,128)(2,1)}, bf16[128,512]{1,0:T(8,128)(2,1)}) custom-call(bf16[384,1024]{1,0:T(8,128)(2,1)S(1)} %pad_maximum_fusion.10.collect_ref, bf16[1024,1024]{1,0:T(8,128)(2,1)} %bitcast.52.table_ref, f32[128,512]{1,0:T(8,128)S(1)} %convolution_add_fusion.mixed_late_ref, f32[128,512]{1,0:T(8,128)S(1)} %fusion.40.tokens_late_ref), custom_call_target="tpu_custom_call" | custom-call | tf_op jit(solution)/shard_map/pallas_call | solution.py:208
  (177 shorter events, 76.2 us)
Async XLA Ops:
  6.6 36.6 %all-to-all-start = ((bf16[32,32,1024]{2,1,0:T(8,128)(2,1)}), bf16[32,32,1024]{2,1,0:T(8,128)(2,1)}, u32[]{:S(2)}, u32[]{:S(2)}) async-start(bf16[32,32,1024]{2,1,0:T(8,128)(2,1)} %bitcast.8), calls=%async_computation | async-start | bytes 4194304 | tf_op jit(solution)/shard_map/all_to_all | solution.py:28
  48.7 6.9 %collective-permute-start = (bf16[8,128,1024]{2,1,0:T(8,128)(2,1)}, bf16[8,128,1024]{2,1,0:T(8,128)(2,1)}, u32[]{:S(2)}, u32[]{:S(2)}) collective-permute-start(bf16[8,128,1024]{2,1,0:T(8,128)(2,1)} %shard_map.94), channel_id=1, source_target_pairs={{0,32},{32,0},{64,96},{96,64},{128,160},{160,128},{192,224},{224,1... | collective-permute-start | bytes 6291464 | tf_op jit(solution)/shard_map/ppermute | solution.py:42
  48.7 48.8 %all-to-all-start.1 = ((bf16[16,192,512]{2,1,0:T(8,128)(2,1)}), bf16[16,192,512]{2,1,0:T(8,128)(2,1)}, u32[]{:S(2)}, u32[]{:S(2)}) async-start(bf16[16,192,512]{2,1,0:T(8,128)(2,1)} %pad_maximum_fusion), calls=%async_computation.1 | async-start | bytes 6291456 | tf_op jit(solution)/shard_map/all_to_all | solution.py:32
  59.0 12.3 %collective-permute-start.2 = (bf16[128,1024]{1,0:T(8,128)(2,1)S(1)}, bf16[128,1024]{1,0:T(8,128)(2,1)S(1)}, u32[]{:S(2)}, u32[]{:S(2)}) collective-permute-start(bf16[128,1024]{1,0:T(8,128)(2,1)S(1)} %get-tuple-element.49), channel_id=1, source_target_pairs={{0,64},{32,96},{64,128},{96,160},{128,192},{160,224},{192,0},{224,... | collective-permute-start | bytes 786440 | tf_op jit(solution)/shard_map/ppermute | solution.py:42
  62.3 15.3 %collective-permute-start.3 = (bf16[128,1024]{1,0:T(8,128)(2,1)S(1)}, bf16[128,1024]{1,0:T(8,128)(2,1)S(1)}, u32[]{:S(2)}, u32[]{:S(2)}) collective-permute-start(bf16[128,1024]{1,0:T(8,128)(2,1)S(1)} %get-tuple-element.50), channel_id=1, source_target_pairs={{0,192},{32,224},{64,0},{96,32},{128,64},{160,96},{192,128},{224,1... | collective-permute-start | bytes 786440 | tf_op jit(solution)/shard_map/ppermute | solution.py:42
  64.5 25.9 %collective-permute-start.1 = (bf16[128,1024]{1,0:T(8,128)(2,1)}, bf16[128,1024]{1,0:T(8,128)(2,1)}, u32[]{:S(2)}, u32[]{:S(2)}) collective-permute-start(bf16[128,1024]{1,0:T(8,128)(2,1)} %get-tuple-element.47), channel_id=1, source_target_pairs={{0,192},{32,224},{64,0},{96,32},{128,64},{160,96},{192,128},{224,1... | collective-permute-start | bytes 786440 | tf_op jit(solution)/shard_map/ppermute | solution.py:42
  78.6 11.9 %collective-permute-start.4 = (bf16[128,1024]{1,0:T(8,128)(2,1)}, bf16[128,1024]{1,0:T(8,128)(2,1)}, u32[]{:S(2)}, u32[]{:S(2)}) collective-permute-start(bf16[128,1024]{1,0:T(8,128)(2,1)} %get-tuple-element.54), channel_id=1, source_target_pairs={{0,64},{32,96},{64,128},{96,160},{128,192},{160,224},{192,0},{224,... | collective-permute-start | bytes 786440 | tf_op jit(solution)/shard_map/ppermute | solution.py:42
  86.2 22.6 %collective-permute-start.5 = (bf16[128,1024]{1,0:T(8,128)(2,1)}, bf16[128,1024]{1,0:T(8,128)(2,1)}, u32[]{:S(2)}, u32[]{:S(2)}) collective-permute-start(bf16[128,1024]{1,0:T(8,128)(2,1)} %copy-done.18), channel_id=1, source_target_pairs={{0,64},{32,96},{64,128},{96,160},{128,192},{160,224},{192,0},{224,... | collective-permute-start | bytes 786440 | tf_op jit(solution)/shard_map/ppermute | solution.py:42
  86.6 22.2 %collective-permute-start.6 = (bf16[128,1024]{1,0:T(8,128)(2,1)}, bf16[128,1024]{1,0:T(8,128)(2,1)}, u32[]{:S(2)}, u32[]{:S(2)}) collective-permute-start(bf16[128,1024]{1,0:T(8,128)(2,1)} %get-tuple-element.57), channel_id=1, source_target_pairs={{0,192},{32,224},{64,0},{96,32},{128,64},{160,96},{192,128},{224,1... | collective-permute-start | bytes 786440 | tf_op jit(solution)/shard_map/ppermute | solution.py:42
  98.4 8.5 %collective-permute-start.7 = (bf16[128,512]{1,0:T(8,128)(2,1)S(1)}, bf16[128,512]{1,0:T(8,128)(2,1)S(1)}, u32[]{:S(2)}, u32[]{:S(2)}) collective-permute-start(bf16[128,512]{1,0:T(8,128)(2,1)S(1)} %dynamic-slice_bitcast_fusion), channel_id=1, source_target_pairs={{0,16},{1,17},{2,18},{3,19},{4,20},{5,21},{6,22},{7,23},{8,24},{9,... | collective-permute-start | bytes 393224 | tf_op jit(solution)/shard_map/ppermute | solution.py:38
  108.5 2.3 %collective-permute-start.8 = (bf16[2,32,512]{2,1,0:T(8,128)(2,1)S(1)}, bf16[2,32,512]{2,1,0:T(8,128)(2,1)S(1)}, u32[]{:S(2)}, u32[]{:S(2)}) collective-permute-start(bf16[2,32,512]{2,1,0:T(8,128)(2,1)S(1)} %fusion.18), channel_id=1, source_target_pairs={{0,32},{32,0},{64,96},{96,64},{128,160},{160,128},{192,224},{224,1... | collective-permute-start | bytes 196616 | tf_op jit(solution)/shard_map/ppermute | solution.py:42
  111.5 8.0 %collective-permute-start.11 = (bf16[2,32,512]{2,1,0:T(8,128)(2,1)}, bf16[2,32,512]{2,1,0:T(8,128)(2,1)}, u32[]{:S(2)}, u32[]{:S(2)}) collective-permute-start(bf16[2,32,512]{2,1,0:T(8,128)(2,1)} %fusion.13), channel_id=1, source_target_pairs={{0,192},{32,224},{64,0},{96,32},{128,64},{160,96},{192,128},{224,1... | collective-permute-start | bytes 196616 | tf_op jit(solution)/shard_map/ppermute | solution.py:42
  114.9 10.6 %collective-permute-start.10 = (bf16[2,32,512]{2,1,0:T(8,128)(2,1)}, bf16[2,32,512]{2,1,0:T(8,128)(2,1)}, u32[]{:S(2)}, u32[]{:S(2)}) collective-permute-start(bf16[2,32,512]{2,1,0:T(8,128)(2,1)} %fusion.13), channel_id=1, source_target_pairs={{0,128},{32,160},{64,192},{96,224},{128,0},{160,32},{192,64},{224,... | collective-permute-start | bytes 196616 | tf_op jit(solution)/shard_map/ppermute | solution.py:42
  117.6 7.9 %collective-permute-start.9 = (bf16[2,32,512]{2,1,0:T(8,128)(2,1)}, bf16[2,32,512]{2,1,0:T(8,128)(2,1)}, u32[]{:S(2)}, u32[]{:S(2)}) collective-permute-start(bf16[2,32,512]{2,1,0:T(8,128)(2,1)} %fusion.13), channel_id=1, source_target_pairs={{0,64},{32,96},{64,128},{96,160},{128,192},{160,224},{192,0},{224,... | collective-permute-start | bytes 196616 | tf_op jit(solution)/shard_map/ppermute | solution.py:42
  129.3 6.6 %collective-permute-start.17 = (bf16[128,512]{1,0:T(8,128)(2,1)S(1)}, bf16[128,512]{1,0:T(8,128)(2,1)S(1)}, u32[]{:S(2)}, u32[]{:S(2)}) collective-permute-start(bf16[128,512]{1,0:T(8,128)(2,1)S(1)} %pad_maximum_fusion.12), channel_id=1, source_target_pairs={{0,16},{1,17},{2,18},{3,19},{4,20},{5,21},{6,22},{7,23},{8,24},{9,... | collective-permute-start | bytes 393224 | tf_op jit(solution)/shard_map/ppermute | solution.py:38
  131.6 6.5 %collective-permute-start.18 = (bf16[2,128,1024]{2,1,0:T(8,128)(2,1)}, bf16[2,128,1024]{2,1,0:T(8,128)(2,1)}, u32[]{:S(2)}, u32[]{:S(2)}) collective-permute-start(bf16[2,128,1024]{2,1,0:T(8,128)(2,1)} %pad_maximum_fusion.11), channel_id=1, source_target_pairs={{0,32},{32,0},{64,96},{96,64},{128,160},{160,128},{192,224},{224,1... | collective-permute-start | bytes 1572872 | tf_op jit(solution)/shard_map/ppermute | solution.py:42
  132.1 27.4 %collective-permute-start.14 = (bf16[2,128,1024]{2,1,0:T(8,128)(2,1)}, bf16[2,128,1024]{2,1,0:T(8,128)(2,1)S(1)}, u32[]{:S(2)}, u32[]{:S(2)}) collective-permute-start(bf16[2,128,1024]{2,1,0:T(8,128)(2,1)} %pad_maximum_fusion.11), channel_id=1, source_target_pairs={{0,192},{32,224},{64,0},{96,32},{128,64},{160,96},{192,128},{224,1... | collective-permute-start | bytes 1572872 | tf_op jit(solution)/shard_map/ppermute | solution.py:42
  134.1 26.9 %collective-permute-start.13 = (bf16[2,128,1024]{2,1,0:T(8,128)(2,1)}, bf16[2,128,1024]{2,1,0:T(8,128)(2,1)}, u32[]{:S(2)}, u32[]{:S(2)}) collective-permute-start(bf16[2,128,1024]{2,1,0:T(8,128)(2,1)} %pad_maximum_fusion.11), channel_id=1, source_target_pairs={{0,64},{32,96},{64,128},{96,160},{128,192},{160,224},{192,0},{224,... | collective-permute-start | bytes 1572872 | tf_op jit(solution)/shard_map/ppermute | solution.py:42
  138.0 55.9 %all-to-all-start.2 = ((bf16[16,192,512]{2,1,0:T(8,128)(2,1)}), bf16[16,192,512]{2,1,0:T(8,128)(2,1)}, u32[]{:S(2)}, u32[]{:S(2)}) async-start(bf16[16,192,512]{2,1,0:T(8,128)(2,1)} %pad_maximum_fusion.1), calls=%async_computation.2 | async-start | bytes 6291456 | tf_op jit(solution)/shard_map/all_to_all | solution.py:32
  163.1 7.7 %collective-permute-start.19 = (bf16[2,2,128,1024]{3,2,1,0:T(8,128)(2,1)S(1)}, bf16[2,2,128,1024]{3,2,1,0:T(8,128)(2,1)S(1)}, u32[]{:S(2)}, u32[]{:S(2)}) collective-permute-start(bf16[2,2,128,1024]{3,2,1,0:T(8,128)(2,1)S(1)} %pad_maximum_fusion.7), channel_id=1, source_target_pairs={{0,32},{32,0},{64,96},{96,64},{128,160},{160,128},{192,224},{224,1... | collective-permute-start | bytes 3145736 | tf_op jit(solution)/shard_map/ppermute | solution.py:42
  163.2 11.1 %collective-permute-start.15 = (bf16[128,1024]{1,0:T(8,128)(2,1)S(1)}, bf16[128,1024]{1,0:T(8,128)(2,1)S(1)}, u32[]{:S(2)}, u32[]{:S(2)}) collective-permute-start(bf16[128,1024]{1,0:T(8,128)(2,1)S(1)} %slice_bitcast_fusion.1), channel_id=1, source_target_pairs={{0,64},{32,96},{64,128},{96,160},{128,192},{160,224},{192,0},{224,... | collective-permute-start | bytes 786440 | tf_op jit(solution)/shard_map/ppermute | solution.py:42
  163.8 12.1 %collective-permute-start.16 = (bf16[128,1024]{1,0:T(8,128)(2,1)S(1)}, bf16[128,1024]{1,0:T(8,128)(2,1)S(1)}, u32[]{:S(2)}, u32[]{:S(2)}) collective-permute-start(bf16[128,1024]{1,0:T(8,128)(2,1)S(1)} %slice_bitcast_fusion), channel_id=1, source_target_pairs={{0,192},{32,224},{64,0},{96,32},{128,64},{160,96},{192,128},{224,1... | collective-permute-start | bytes 786440 | tf_op jit(solution)/shard_map/ppermute | solution.py:42
  175.9 2.2 collective-permute-start.20
  195.5 30.7 %all-to-all-start.3 = ((bf16[32,32,1024]{2,1,0:T(8,128)(2,1)}), bf16[32,32,1024]{2,1,0:T(8,128)(2,1)}, u32[]{:S(2)}, u32[]{:S(2)}) async-start(bf16[32,32,1024]{2,1,0:T(8,128)(2,1)} %bitcast.51), calls=%async_computation.3 | async-start | bytes 4194304 | tf_op jit(solution)/shard_map/all_to_all | solution.py:28
  (34 other events, 128.9 us)
